TPU v7x, 32 devices: a whole 2x2x4 slice. The times are simulated.
32 devices in a mesh: groups: 2 (over x), tok: 4 (over y, core), hid: 4 (over z).
Axes of the slice: x: 2, y: 2, z: 4, core: 2. Of those that a mesh axis runs over, the one named last changes fastest.
Arguments:
- tokens: bfloat16 [2048, 5376], P(('groups', 'tok'), 'hid'), parts along dimension 0, may hold values from -6 to 6
- w_query: bfloat16 [5376, 2048], P('tok', 'hid'), may hold values from -0.078125 to 0.078125
- key_weight: bfloat16 [5376, 1024], P('tok', 'hid'), may hold values from -0.078125 to 0.078125
- value_weight: bfloat16 [5376, 1024], P('tok', 'hid'), may hold values from -0.078125 to 0.078125
- w_out: bfloat16 [2048, 5376], P('tok', 'hid'), may hold values from -0.5 to 0.5
- query_norm_gain: float32 [128], replicated, may hold values from 0.5 to 2
- key_gain: float32 [128], replicated, may hold values from 0.5 to 2
- positions: int32 [2048], P('groups'), parts along dimension 0, may hold values from 0 to 131071, as said below
- grad_out: bfloat16 [2048, 5376], P(('groups', 'tok'), 'hid'), parts along dimension 0, may hold values from -6 to 6
Outputs:
- attn_out: bfloat16 [2048, 5376], P(('groups', 'tok'), 'hid'), parts along dimension 0
- grad_x: bfloat16 [2048, 5376], P(('groups', 'tok'), 'hid'), parts along dimension 0
- grad_wq: float32 [10752, 2048], P(('groups', 'tok'), 'hid'), parts along dimension 0
- key_weight_gradient: float32 [10752, 1024], P(('groups', 'tok'), 'hid'), parts along dimension 0
- value_weight_gradient: float32 [10752, 1024], P(('groups', 'tok'), 'hid'), parts along dimension 0
- grad_wo: float32 [4096, 5376], P(('groups', 'tok'), 'hid'), parts along dimension 0
There are 2 independent parts, one for each index of `groups`. A program takes and returns all parts, laid end to end along the dimension named above; an argument that names none is the same for every part. Nothing has to cross between parts.
Inputs may be any that keep to these rules, and one draw needn't show every extreme that they name: positions[t] is token t's position in its document: it rises by one from token to token and is 0 where a document begins; the first document begins before the window and its last token in the window has position 131071; at least one document begins inside the window.
All inputs are finite; a program needn't handle non-finite values.
Results may differ from a plain program's by a relative error of at most 0.02.
Values may be sent and summed in bfloat16 or wider, within the bound.
A program may use at most 192 MiB of HBM per device.

v0:
```python
import jax
import jax.numpy as jnp
from jax import lax
from jax.sharding import PartitionSpec as P

QUERY_HEADS = 16
KEY_VALUE_HEADS = 8
HEAD_SIZE = 128
WINDOW = 1024
TOK_DEV = 256


attn_scale = 168.0 ** (-0.5)
rope_base = 10000.0
norm_eps = 1e-06


def shifted(value, axis, steps):
    count = lax.axis_size(axis)
    first, last = (max(0, -steps), min(count, count - steps))
    return lax.ppermute(value, axis, [(source, source + steps) for source in range(first, last)])


def swapped(value, axis, bit):
    count = lax.axis_size(axis)
    return lax.ppermute(value, axis, [(source, source ^ bit) for source in range(count)])


def gather_swapped(value, axis):
    count = lax.axis_size(axis)
    held = {0: value}
    bit = count // 2
    while bit:
        for offset in list(held):
            held[offset ^ bit] = swapped(held[offset], axis, bit)
        bit //= 2
    return [held[offset] for offset in range(count)]


def begin_scatter(left, right, axis):
    count = lax.axis_size(axis)
    index = lax.axis_index(axis)
    height = left.shape[1] // count

    def product(offset):
        picked = lax.dynamic_slice_in_dim(left, (index ^ offset) * height, height, 1)
        return jnp.einsum("td,tc->dc", picked, right, preferred_element_type=jnp.float32)

    totals = {}
    for offset in range(count - 2, -1, -2):
        arrived = swapped(product(offset ^ 1).astype(jnp.bfloat16), axis, 1)
        totals[offset] = product(offset) + arrived.astype(jnp.float32)
        if offset:
            totals[offset] = totals[offset].astype(jnp.bfloat16)
    return totals


def finish_scatter(totals, axis):
    count = lax.axis_size(axis)
    totals = dict(totals)
    bit = 2
    while bit < count:
        for offset in range(count - bit, 0, -2 * bit):
            arrived = swapped(totals[offset], axis, bit).astype(jnp.float32)
            kept = offset ^ bit
            total = totals[kept].astype(jnp.float32) + arrived
            totals[kept] = total.astype(jnp.bfloat16) if kept else total
        bit *= 2
    return totals[0]


def ordered(value, *groups):
    sent = [{key: total for key, total in group.items() if key} for group in groups]
    value, sent = lax.optimization_barrier((value, sent))
    return value, [{**group, **part} for group, part in zip(groups, sent)]


def rotary_tables(token_pos):
    half_dim = HEAD_SIZE // 2
    freqs = rope_base ** (-jnp.arange(half_dim, dtype=jnp.float32) * 2.0 / HEAD_SIZE)
    angles = token_pos.astype(jnp.float32)[:, None] * freqs[None, :]
    return (jnp.cos(angles), jnp.sin(angles))


def prepare_inputs(raw_values, gain_vector, cosine_table, sine_table):
    scaled = (
        raw_values
        * lax.rsqrt(jnp.mean(raw_values * raw_values, -1, keepdims=True) + norm_eps)
        * gain_vector
    )
    half_dim = scaled.shape[-1] // 2
    first_half = scaled[..., :half_dim]
    second_half = scaled[..., half_dim:]
    cos_rows = cosine_table[:, None, :]
    sin_rows = sine_table[:, None, :]
    return jnp.concatenate(
        [
            first_half * cos_rows - second_half * sin_rows,
            second_half * cos_rows + first_half * sin_rows,
        ],
        -1,
    )


def local(
    tokens, w_query, key_weight, value_weight, w_out, query_norm_gain, key_gain, positions, grad_out
):
    hidden_count = lax.axis_size("hid")
    block_index = lax.axis_index("tok")
    query_heads = QUERY_HEADS // hidden_count
    key_value_heads = KEY_VALUE_HEADS // hidden_count
    group_width = QUERY_HEADS // KEY_VALUE_HEADS
    reach = min(WINDOW // TOK_DEV, lax.axis_size("tok") - 1)
    span_rows = (reach + 1) * TOK_DEV
    leading_part = reach * TOK_DEV
    first_token = block_index * TOK_DEV
    query_cols = query_heads * HEAD_SIZE
    kv_cols = key_value_heads * HEAD_SIZE
    full_rows = lax.all_gather(tokens, "hid", axis=1, tiled=True)
    query_pieces = gather_swapped(w_query, "tok")
    kv_pieces = gather_swapped(jnp.concatenate([key_weight, value_weight], 1), "tok")
    full_wo = lax.all_gather(w_out, "tok", axis=0, tiled=True)
    height = w_query.shape[0]

    def project(pieces):
        total = 0.0
        for offset, piece in enumerate(pieces):
            start = (block_index ^ offset) * height
            columns = lax.dynamic_slice_in_dim(full_rows, start, height, 1)
            total = total + jnp.dot(columns, piece, preferred_element_type=jnp.float32)
        return total

    kv_unnormed = project(kv_pieces)
    query_unnormed = project(query_pieces)
    key_unnormed = kv_unnormed[:, :kv_cols]
    value_raw = kv_unnormed[:, kv_cols:]
    partial_heads = jnp.einsum("td,hd->th", grad_out, full_wo, preferred_element_type=jnp.float32)
    attended_gradient = lax.psum_scatter(
        partial_heads.astype(jnp.bfloat16), "hid", scatter_dimension=1, tiled=True
    )
    values_local = value_raw.astype(jnp.bfloat16)
    token_pos = lax.dynamic_slice_in_dim(positions, first_token, TOK_DEV, 0)
    cosine_table, sine_table = rotary_tables(token_pos)
    query_heads_raw = query_unnormed.reshape(TOK_DEV, query_heads, HEAD_SIZE)
    key_heads_raw = key_unnormed.reshape(TOK_DEV, key_value_heads, HEAD_SIZE)
    query_rows = (
        prepare_inputs(query_heads_raw, query_norm_gain, cosine_table, sine_table)
        .astype(jnp.bfloat16)
        .reshape(TOK_DEV, key_value_heads, group_width, HEAD_SIZE)
    )
    keys_local = prepare_inputs(key_heads_raw, key_gain, cosine_table, sine_table).astype(
        jnp.bfloat16
    )
    key_value = jnp.concatenate([keys_local.reshape(TOK_DEV, kv_cols), values_local], 1)
    blocks = [shifted(key_value, "tok", steps) for steps in range(reach, 0, -1)] + [key_value]
    window = jnp.concatenate(blocks, 0)
    key_window = window[:, :kv_cols].reshape(span_rows, key_value_heads, HEAD_SIZE)
    value_window = window[:, kv_cols:].reshape(span_rows, key_value_heads, HEAD_SIZE)
    query_index = first_token + jnp.arange(TOK_DEV, dtype=jnp.int32)
    key_index = first_token - leading_part + jnp.arange(span_rows, dtype=jnp.int32)
    padded_pos = jnp.pad(positions, (leading_part, 0))
    key_pos = lax.dynamic_slice_in_dim(padded_pos, first_token, span_rows, 0)
    distance = query_index[:, None] - key_index[None, :]
    allowed = (
        (key_index[None, :] >= 0)
        & (distance >= 0)
        & (distance < WINDOW)
        & (token_pos[:, None] - key_pos[None, :] == distance)
    )
    scores = (
        jnp.einsum("tkgd,ukd->kgtu", query_rows, key_window, preferred_element_type=jnp.float32)
        * attn_scale
    )
    weights = jnp.where(allowed[None, None], jnp.exp(scores), 0.0)
    probabilities = weights / jnp.sum(weights, -1, keepdims=True)
    rounded = probabilities.astype(jnp.bfloat16)
    attended = jnp.einsum(
        "kgtu,ukd->tkgd", rounded, value_window, preferred_element_type=jnp.float32
    )
    attended = attended.astype(jnp.bfloat16).reshape(TOK_DEV, query_cols)
    attended, attended_gradient = lax.optimization_barrier((attended, attended_gradient))
    all_heads = lax.all_gather(attended, "hid", axis=1, tiled=True)
    output = jnp.dot(all_heads, full_wo, preferred_element_type=jnp.float32)
    attn_out = output.astype(jnp.bfloat16)
    attended_gradient = attended_gradient.reshape(TOK_DEV, key_value_heads, group_width, HEAD_SIZE)
    grad_probs = jnp.einsum(
        "tkgd,ukd->kgtu", attended_gradient, value_window, preferred_element_type=jnp.float32
    )
    grad_scores = (
        attn_scale
        * probabilities
        * (grad_probs - jnp.sum(probabilities * grad_probs, -1, keepdims=True))
    )
    grad_scores = grad_scores.astype(jnp.bfloat16)
    grad_queries = jnp.einsum(
        "kgtu,ukd->tkgd", grad_scores, key_window, preferred_element_type=jnp.float32
    )
    keys_gradient = jnp.einsum(
        "kgtu,tkgd->ukd", grad_scores, query_rows, preferred_element_type=jnp.float32
    )
    values_gradient = jnp.einsum(
        "kgtu,tkgd->ukd", rounded, attended_gradient, preferred_element_type=jnp.float32
    )
    grad_window = jnp.concatenate(
        [keys_gradient.reshape(span_rows, kv_cols), values_gradient.reshape(span_rows, kv_cols)], 1
    )
    grad_kv = grad_window[leading_part:]
    for steps in range(reach, 0, -1):
        start = (reach - steps) * TOK_DEV
        block = grad_window[start : start + TOK_DEV].astype(jnp.bfloat16)
        grad_kv = grad_kv + shifted(block, "tok", -steps).astype(jnp.float32)
    _, query_pull = jax.vjp(
        lambda raw_values: prepare_inputs(raw_values, query_norm_gain, cosine_table, sine_table),
        query_heads_raw,
    )
    _, key_pullback = jax.vjp(
        lambda raw_values: prepare_inputs(raw_values, key_gain, cosine_table, sine_table),
        key_heads_raw,
    )
    query_back = (
        query_pull(grad_queries.reshape(TOK_DEV, query_heads, HEAD_SIZE))[0]
        .astype(jnp.bfloat16)
        .reshape(TOK_DEV, query_cols)
    )
    key_backward = (
        key_pullback(grad_kv[:, :kv_cols].reshape(TOK_DEV, key_value_heads, HEAD_SIZE))[0]
        .astype(jnp.bfloat16)
        .reshape(TOK_DEV, kv_cols)
    )
    value_backward = grad_kv[:, kv_cols:].astype(jnp.bfloat16)
    kv_back = jnp.concatenate([key_backward, value_backward], 1)
    query_sums = begin_scatter(full_rows, query_back, "tok")
    out_sums = begin_scatter(all_heads, grad_out, "tok")
    kv_back, (query_sums, out_sums) = ordered(kv_back, query_sums, out_sums)
    block_rows = jnp.zeros((TOK_DEV, full_rows.shape[1]), jnp.bfloat16)
    for offset in range(len(query_pieces)):
        product = jnp.einsum(
            "tc,dc->td", query_back, query_pieces[offset], preferred_element_type=jnp.float32
        ) + jnp.einsum("tc,dc->td", kv_back, kv_pieces[offset], preferred_element_type=jnp.float32)
        start = (block_index ^ offset) * height
        block_rows = lax.dynamic_update_slice_in_dim(
            block_rows, product.astype(jnp.bfloat16), start, 1
        )
    grad_x = lax.psum_scatter(block_rows, "hid", scatter_dimension=1, tiled=True)
    kv_sums = begin_scatter(full_rows, kv_back, "tok")
    grad_wq = finish_scatter(query_sums, "tok")
    grad_wo = finish_scatter(out_sums, "tok")
    grad_wkv = finish_scatter(kv_sums, "tok")
    key_weight_gradient = grad_wkv[:, :kv_cols]
    value_weight_gradient = grad_wkv[:, kv_cols:]
    return (attn_out, grad_x, grad_wq, key_weight_gradient, value_weight_gradient, grad_wo)


def solution(mesh):
    return jax.shard_map(
        local,
        mesh=mesh,
        in_specs=(
            P(("groups", "tok"), "hid"),
            P("tok", "hid"),
            P("tok", "hid"),
            P("tok", "hid"),
            P("tok", "hid"),
            P(),
            P(),
            P("groups"),
            P(("groups", "tok"), "hid"),
        ),
        out_specs=(
            P(("groups", "tok"), "hid"),
            P(("groups", "tok"), "hid"),
            P(("groups", "tok"), "hid"),
            P(("groups", "tok"), "hid"),
            P(("groups", "tok"), "hid"),
            P(("groups", "tok"), "hid"),
        ),
        check_vma=False,
    )
```

profile of v0, /device:TPU:0, one launch (start us, length us, event | category | flops | bytes accessed | tf_op | source)
XLA Modules:
  0.0 346.8 jit_solution(17867085953432618702)
XLA Ops:
  10.5 3.0 collective-permute-start.1
  14.2 30.6 %collective-permute-done.1 = bf16[1344,512]{1,0:T(8,128)(2,1)} collective-permute-done((bf16[1344,512]{1,0:T(8,128)(2,1)}, bf16[1344,512]{1,0:T(8,128)(2,1)}, u32[]{:S(2)}, u32[]{:S(2)}) %collective-permute-start.1) | collective-permute-done | bytes 1376288 | tf_op jit(solution)/shard_map/ppermute | solution.py:26
  47.6 25.9 %collective-permute-done.7 = bf16[1344,512]{1,0:T(8,128)(2,1)} collective-permute-done((bf16[1344,512]{1,0:T(8,128)(2,1)}, bf16[1344,512]{1,0:T(8,128)(2,1)}, u32[]{:S(2)}, u32[]{:S(2)}) %collective-permute-start.7) | collective-permute-done | bytes 1376288 | tf_op jit(solution)/shard_map/ppermute | solution.py:26
  73.5 2.1 fusion.52
  75.7 2.5 convolution_add_fusion.9
  78.6 2.3 convolution_add_fusion.8
  81.0 1.9 convolution_add_fusion.7
  84.4 1.8 reshape.229
  86.2 2.0 multiply_reduce_fusion.3
  94.9 2.9 collective-permute-start.5
  97.9 3.6 %collective-permute-start.4 = (bf16[256,512]{1,0:T(8,128)(2,1)}, bf16[256,512]{1,0:T(8,128)(2,1)}, u32[]{:S(2)}, u32[]{:S(2)}) collective-permute-start(bf16[256,512]{1,0:T(8,128)(2,1)} %pad_maximum_fusion.1), channel_id=1, source_target_pairs={{0,8},{4,12},{1,9},{5,13},{2,10},{6,14},{3,11},{7,15},{16,24},{20,... | collective-permute-start | bytes 786440 | tf_op jit(solution)/shard_map/ppermute | solution.py:21
  101.5 2.0 collective-permute-start.3
  103.5 1.9 fusion.50
  105.5 1.9 convolution_add_fusion.6
  107.4 1.9 convolution_add_fusion.5
  109.4 2.7 convolution_add_fusion.4
  112.1 2.0 reshape.232
  114.1 2.0 multiply_reduce_fusion.1
  117.2 5.3 %convolution_convert_fusion.7 = bf16[256,2048]{1,0:T(8,128)(2,1)} fusion(bf16[256,1344]{0,1:T(8,128)(2,1)S(1)} %copy-done, bf16[2048,1344]{0,1:T(8,128)(2,1)} %all-gather.6.cloned.1.call-done), kind=kOutput, calls=%fused_computation.33 | convolution fusion | flops 1409810432 | bytes 7241728 | tf_op jit(solution)/shard_map/td,hd->th/dot_general | solution.py:137
  130.3 2.0 reshape.230
  132.3 2.0 reshape.231
  134.2 2.0 copy.82
  136.2 2.7 fusion.4
  138.9 2.1 copy-done.16
  141.0 1.9 convolution_convert_fusion.8
  142.8 9.2 %reduce-scatter.3.cloned.1.call-done = bf16[256,512]{1,0:T(8,128)(2,1)} async-done(((bf16[256,2048]{1,0:T(8,128)(2,1)}), bf16[256,512]{1,0:T(8,128)(2,1)}) %reduce-scatter.3.cloned.1.call-update) | async-done | bytes 262160 | tf_op jit(solution)/shard_map/reduce_scatter | solution.py:138
  152.0 1.8 copy.103
  153.8 4.0 %fusion = (f32[2,2,256]{2,1,0:T(2,128)S(1)}, f32[2,1024,256,2]{2,1,3,0:T(8,128)S(1)}) fusion(f32[2,2,256]{2,1,0:T(2,128)S(1)} %get-tuple-element.39, f32[2,1024,256,2]{2,1,3,0:T(8,128)} %copy-done.16, pred[256,1024]{0,1:T(8,128)(4,1)} %fusion.17, bf16[256,2,2,128]{0,3,2,1:T(8,128)(2,1)} %bitcast.140, bf16[1024,2,128,1]{2,1,0,3:T(2,128)(2,1)} %bitcast.136), kind=kOutput, calls=%fused_computation.2 | convolution fusion | flops 273677312 | bytes 9445376 | tf_op jit(solution)/shard_map/tkgd,ukd->kgtu/dot_general | solution.py:186
  160.4 1.8 fusion.80
  162.3 2.4 fusion.14
  164.7 1.9 fusion.112
  166.6 1.9 copy.100
  168.5 1.9 copy.99
  170.5 1.6 multiply_add_fusion.1
  176.2 1.8 fusion.13
  185.2 3.0 fusion.62
  188.2 4.1 %collective-permute-done.10 = bf16[256,512]{0,1:T(8,128)(2,1)S(1)} collective-permute-done((bf16[256,512]{0,1:T(8,128)(2,1)S(1)}, bf16[256,512]{0,1:T(8,128)(2,1)S(1)}, u32[]{:S(2)}, u32[]{:S(2)}) %collective-permute-start.10) | collective-permute-done | bytes 262176 | tf_op jit(solution)/shard_map/ppermute | solution.py:21
  192.3 2.0 collective-permute-done.9
  196.0 2.6 convolution_convert_fusion.4
  199.3 1.6 slice.108
  200.9 1.7 copy.102
  202.7 1.7 copy.101
  206.6 2.2 multiply_reduce_fusion.2
  210.7 2.7 fusion.54
  213.4 1.7 copy.98
  216.1 3.1 add_convert_fusion.2
  219.2 3.1 add_convert_fusion.1
  222.2 1.8 broadcast_in_dim.16
  224.1 2.7 fusion.12
  226.8 1.8 fusion.115
  228.7 1.9 fusion.116
  230.6 1.9 fusion.117
  232.5 2.8 fusion.6
  235.3 2.8 fusion.8
  238.1 2.8 fusion.10
  240.9 1.6 convolution_convert_fusion.3
  246.9 2.5 convolution_convert_fusion.6
  249.4 2.0 collective-permute-start.20
  253.2 26.7 %collective-permute-done.15 = bf16[1344,512]{1,0:T(8,128)(2,1)S(1)} collective-permute-done((bf16[1344,512]{1,0:T(8,128)(2,1)S(1)}, bf16[1344,512]{1,0:T(8,128)(2,1)S(1)}, u32[]{:S(2)}, u32[]{:S(2)}) %collective-permute-start.15) | collective-permute-done | bytes 1376288 | tf_op jit(solution)/shard_map/ppermute | solution.py:26
  279.9 2.1 convert_add_fusion.2
  282.0 27.4 %collective-permute-done.20 = bf16[512,1344]{0,1:T(8,128)(2,1)S(1)} collective-permute-done((bf16[512,1344]{0,1:T(8,128)(2,1)S(1)}, bf16[512,1344]{0,1:T(8,128)(2,1)S(1)}, u32[]{:S(2)}, u32[]{:S(2)}) %collective-permute-start.20) | collective-permute-done | bytes 1376288 | tf_op jit(solution)/shard_map/ppermute | solution.py:26
  309.4 2.1 convert_add_fusion
  311.5 26.5 %collective-permute-done.18 = bf16[1344,512]{1,0:T(8,128)(2,1)S(1)} collective-permute-done((bf16[1344,512]{1,0:T(8,128)(2,1)S(1)}, bf16[1344,512]{1,0:T(8,128)(2,1)S(1)}, u32[]{:S(2)}, u32[]{:S(2)}) %collective-permute-start.18) | collective-permute-done | bytes 1376288 | tf_op jit(solution)/shard_map/ppermute | solution.py:26
  338.5 1.7 fusion.109
  (188 shorter events, 51.9 us)
Async XLA Ops:
  7.2 110.0 %copy-start = (bf16[256,1344]{0,1:T(8,128)(2,1)S(1)}, bf16[256,1344]{0,1:T(8,128)(2,1)}, u32[]{:S(2)}) copy-start(bf16[256,1344]{0,1:T(8,128)(2,1)} %param.17) | copy-start | bytes 2064388
  7.2 1.6 copy-start.36
  7.2 2.5 copy-start.37
  7.2 66.3 %all-gather.4.cloned.1.call-start = ((), (), s32[]{:S(2)}) async-start(), calls=%async_computation.2 | async-start | bytes 3440640 | tf_op jit(solution)/shard_map/all_gather | solution.py:119
  7.9 6.1 %copy-start.41 = (s32[1024]{0:T(1024)S(1)}, s32[1024]{0:T(1024)}, u32[]{:S(2)}) copy-start(s32[1024]{0:T(1024)} %param.16) | copy-start | bytes 12292
  7.9 109.2 %all-gather.6.cloned.1.call-start = ((), (), s32[]{:S(2)}) async-start(), calls=%async_computation.3 | async-start | bytes 6881280 | tf_op jit(solution)/shard_map/all_gather | solution.py:122
  8.7 143.4 %reduce-scatter.3.cloned.1.call-start = ((), (), s32[]{:S(2)}) async-start(), calls=%async_computation.4 | async-start | bytes 1310720 | tf_op jit(solution)/shard_map/reduce_scatter | solution.py:138
  10.5 34.3 %collective-permute-start.1 = (bf16[1344,512]{1,0:T(8,128)(2,1)}, bf16[1344,512]{1,0:T(8,128)(2,1)}, u32[]{:S(2)}, u32[]{:S(2)}) collective-permute-start(bf16[1344,512]{1,0:T(8,128)(2,1)} %constant_dynamic-update-slice_fusion), channel_id=1, source_target_pairs={{0,8},{4,12},{8,0},{12,4},{1,9},{5,13},{9,1},{13,5},{2,10},{6,14},... | collective-permute-start | bytes 4128776 | tf_op jit(solution)/shard_map/ppermute | solution.py:26
  13.5 60.0 %collective-permute-start.7 = (bf16[1344,512]{1,0:T(8,128)(2,1)}, bf16[1344,512]{1,0:T(8,128)(2,1)}, u32[]{:S(2)}, u32[]{:S(2)}) collective-permute-start(bf16[1344,512]{1,0:T(8,128)(2,1)} %param.10), channel_id=1, source_target_pairs={{0,8},{4,12},{8,0},{12,4},{1,9},{5,13},{9,1},{13,5},{2,10},{6,14},... | collective-permute-start | bytes 4128776 | tf_op jit(solution)/shard_map/ppermute | solution.py:26
  13.5 62.1 %collective-permute-start = (bf16[1344,512]{1,0:T(8,128)(2,1)}, bf16[1344,512]{1,0:T(8,128)(2,1)}, u32[]{:S(2)}, u32[]{:S(2)}) collective-permute-start(bf16[1344,512]{1,0:T(8,128)(2,1)} %constant_dynamic-update-slice_fusion), channel_id=1, source_target_pairs={{0,4},{4,0},{8,12},{12,8},{1,5},{5,1},{9,13},{13,9},{2,6},{6,2},{1... | collective-permute-start | bytes 4128776 | tf_op jit(solution)/shard_map/ppermute | solution.py:26
  13.5 91.9 %collective-permute-start.6 = (bf16[1344,512]{1,0:T(8,128)(2,1)}, bf16[1344,512]{1,0:T(8,128)(2,1)}, u32[]{:S(2)}, u32[]{:S(2)}) collective-permute-start(bf16[1344,512]{1,0:T(8,128)(2,1)} %param.10), channel_id=1, source_target_pairs={{0,4},{4,0},{8,12},{12,8},{1,5},{5,1},{9,13},{13,9},{2,6},{6,2},{1... | collective-permute-start | bytes 4128776 | tf_op jit(solution)/shard_map/ppermute | solution.py:26
  44.8 36.1 %collective-permute-start.2 = (bf16[1344,512]{1,0:T(8,128)(2,1)}, bf16[1344,512]{1,0:T(8,128)(2,1)}, u32[]{:S(2)}, u32[]{:S(2)}) collective-permute-start(bf16[1344,512]{1,0:T(8,128)(2,1)} %collective-permute-done.1), channel_id=1, source_target_pairs={{0,4},{4,0},{8,12},{12,8},{1,5},{5,1},{9,13},{13,9},{2,6},{6,2},{1... | collective-permute-start | bytes 4128776 | tf_op jit(solution)/shard_map/ppermute | solution.py:26
  73.5 35.9 %collective-permute-start.8 = (bf16[1344,512]{1,0:T(8,128)(2,1)}, bf16[1344,512]{1,0:T(8,128)(2,1)}, u32[]{:S(2)}, u32[]{:S(2)}) collective-permute-start(bf16[1344,512]{1,0:T(8,128)(2,1)} %collective-permute-done.7), channel_id=1, source_target_pairs={{0,4},{4,0},{8,12},{12,8},{1,5},{5,1},{9,13},{13,9},{2,6},{6,2},{1... | collective-permute-start | bytes 4128776 | tf_op jit(solution)/shard_map/ppermute | solution.py:26
  75.6 3.0 copy-start.1
  81.0 9.0 %copy-start.43 = (f32[128]{0:T(128)S(1)}, f32[128]{0:T(128)}, u32[]{:S(2)}) copy-start(f32[128]{0:T(128)} %param.15) | copy-start | bytes 1540
  92.3 13.2 %copy-start.26 = (bf16[256,256]{1,0:T(8,128)(2,1)}, bf16[256,256]{1,0:T(8,128)(2,1)S(1)}, u32[]{:S(2)}) copy-start(bf16[256,256]{1,0:T(8,128)(2,1)S(1)} %slice.109) | copy-start | bytes 393220
  94.2 7.3 %copy-start.28 = (bf16[32,8,2,128]{3,1,2,0:T(8,128)(2,1)}, bf16[32,8,2,128]{3,1,2,0:T(8,128)(2,1)S(1)}, u32[]{:S(2)}) copy-start(bf16[32,8,2,128]{3,1,2,0:T(8,128)(2,1)S(1)} %copy.145) | copy-start | bytes 393220
  94.9 33.1 %collective-permute-start.5 = (bf16[256,512]{1,0:T(8,128)(2,1)}, bf16[256,512]{1,0:T(8,128)(2,1)}, u32[]{:S(2)}, u32[]{:S(2)}) collective-permute-start(bf16[256,512]{1,0:T(8,128)(2,1)} %pad_maximum_fusion.1), channel_id=1, source_target_pairs={{0,4},{4,8},{8,12},{1,5},{5,9},{9,13},{2,6},{6,10},{10,14},{3,7},{... | collective-permute-start | bytes 786440 | tf_op jit(solution)/shard_map/ppermute | solution.py:21
  97.9 30.1 %collective-permute-start.4 = (bf16[256,512]{1,0:T(8,128)(2,1)}, bf16[256,512]{1,0:T(8,128)(2,1)}, u32[]{:S(2)}, u32[]{:S(2)}) collective-permute-start(bf16[256,512]{1,0:T(8,128)(2,1)} %pad_maximum_fusion.1), channel_id=1, source_target_pairs={{0,8},{4,12},{1,9},{5,13},{2,10},{6,14},{3,11},{7,15},{16,24},{20,... | collective-permute-start | bytes 786440 | tf_op jit(solution)/shard_map/ppermute | solution.py:21
  101.5 26.5 %collective-permute-start.3 = (bf16[256,512]{1,0:T(8,128)(2,1)}, bf16[256,512]{1,0:T(8,128)(2,1)}, u32[]{:S(2)}, u32[]{:S(2)}) collective-permute-start(bf16[256,512]{1,0:T(8,128)(2,1)} %pad_maximum_fusion.1), channel_id=1, source_target_pairs={{0,12},{1,13},{2,14},{3,15},{16,28},{17,29},{18,30},{19,31}} | collective-permute-start | bytes 786440 | tf_op jit(solution)/shard_map/ppermute | solution.py:21
  117.1 6.4 %copy-start.42 = (f32[128]{0:T(128)S(1)}, f32[128]{0:T(128)}, u32[]{:S(2)}) copy-start(f32[128]{0:T(128)} %param.14) | copy-start | bytes 1540
  122.5 73.5 %all-gather.8.cloned.1.call-start = ((), (), s32[]{:S(2)}) async-start(), calls=%async_computation.5 | async-start | bytes 1310720 | tf_op jit(solution)/shard_map/all_gather | solution.py:182
  123.6 4.4 %copy-start.27 = (bf16[256,256]{1,0:T(8,128)(2,1)S(1)}, bf16[256,256]{1,0:T(8,128)(2,1)}, u32[]{:S(2)}) copy-start(bf16[256,256]{1,0:T(8,128)(2,1)} %copy-done.26) | copy-start | bytes 393220
  123.6 4.4 %copy-start.29 = (bf16[32,8,2,128]{3,1,2,0:T(8,128)(2,1)S(1)}, bf16[32,8,2,128]{3,1,2,0:T(8,128)(2,1)}, u32[]{:S(2)}) copy-start(bf16[32,8,2,128]{3,1,2,0:T(8,128)(2,1)} %copy-done.28) | copy-start | bytes 393220
  136.2 4.8 %copy-start.33 = (pred[256,1024]{0,1:T(8,128)(4,1)S(1)}, pred[256,1024]{0,1:T(8,128)(4,1)}, u32[]{:S(2)}) copy-start(pred[256,1024]{0,1:T(8,128)(4,1)} %fusion.17) | copy-start | bytes 786436
  136.2 4.8 %copy-start.39 = (bf16[1024,2,128]{2,1,0:T(2,128)(2,1)S(1)}, bf16[1024,2,128]{2,1,0:T(2,128)(2,1)}, u32[]{:S(2)}) copy-start(bf16[1024,2,128]{2,1,0:T(2,128)(2,1)} %reshape.230) | copy-start | bytes 1572868
  138.9 2.1 copy-start.16
  153.8 4.0 %copy-start.17 = (f32[2,1024,256,2]{2,1,3,0:T(8,128)S(1)}, f32[2,1024,256,2]{2,1,3,0:T(8,128)}, u32[]{:S(2)}) copy-start(f32[2,1024,256,2]{2,1,3,0:T(8,128)} %copy-done.16) | copy-start | bytes 12582916
  153.8 4.0 %copy-start.34 = (pred[256,1024]{0,1:T(8,128)(4,1)S(1)}, pred[256,1024]{0,1:T(8,128)(4,1)}, u32[]{:S(2)}) copy-start(pred[256,1024]{0,1:T(8,128)(4,1)} %fusion.17) | copy-start | bytes 786436
  157.8 1.3 copy-start.20
  159.2 1.3 copy-start.30
  160.4 1.8 copy-start.40
  164.7 175.6 %reduce-scatter.5.cloned.1.call-start = ((), (), s32[]{:S(2)}) async-start(), calls=%async_computation.6 | async-start | bytes 3440640 | tf_op jit(solution)/shard_map/reduce_scatter | solution.py:244
  170.5 2.6 copy-start.7
  176.2 5.8 %copy-start.8 = (f32[256,4,128]{2,1,0:T(4,128)S(1)}, f32[256,4,128]{2,1,0:T(4,128)}, u32[]{:S(2)}) copy-start(f32[256,4,128]{2,1,0:T(4,128)} %reshape.232) | copy-start | bytes 1572868
  176.2 5.8 %copy-start.12 = (f32[256,4,64]{2,1,0:T(4,128)S(1)}, f32[256,4,64]{2,1,0:T(4,128)}, u32[]{:S(2)}) copy-start(f32[256,4,64]{2,1,0:T(4,128)} %copy-done.11) | copy-start | bytes 786436
  176.2 5.9 %copy-start.14 = (f32[256,4,64]{2,1,0:T(4,128)S(1)}, f32[256,4,64]{2,1,0:T(4,128)}, u32[]{:S(2)}) copy-start(f32[256,4,64]{2,1,0:T(4,128)} %copy-done.13) | copy-start | bytes 786436
  176.2 5.9 %copy-start.25 = (f32[256,4]{1,0:T(8,128)S(1)}, f32[256,4]{1,0:T(8,128)}, u32[]{:S(2)}) copy-start(f32[256,4]{1,0:T(8,128)} %copy.56) | copy-start | bytes 12292
  176.2 5.9 %copy-start.38 = (f32[256,4]{1,0:T(8,128)S(1)}, f32[256,4]{1,0:T(8,128)}, u32[]{:S(2)}) copy-start(f32[256,4]{1,0:T(8,128)} %copy.69) | copy-start | bytes 12292
  178.1 10.1 %collective-permute-start.11 = (bf16[256,512]{0,1:T(8,128)(2,1)S(1)}, bf16[256,512]{0,1:T(8,128)(2,1)S(1)}, u32[]{:S(2)}, u32[]{:S(2)}) collective-permute-start(bf16[256,512]{0,1:T(8,128)(2,1)S(1)} %get-tuple-element.23), channel_id=1, source_target_pairs={{4,0},{8,4},{12,8},{5,1},{9,5},{13,9},{6,2},{10,6},{14,10},{7,3},{... | collective-permute-start | bytes 786440 | tf_op jit(solution)/shard_map/ppermute | solution.py:21
  179.4 12.9 %collective-permute-start.10 = (bf16[256,512]{0,1:T(8,128)(2,1)S(1)}, bf16[256,512]{0,1:T(8,128)(2,1)S(1)}, u32[]{:S(2)}, u32[]{:S(2)}) collective-permute-start(bf16[256,512]{0,1:T(8,128)(2,1)S(1)} %get-tuple-element.24), channel_id=1, source_target_pairs={{8,0},{12,4},{9,1},{13,5},{10,2},{14,6},{11,3},{15,7},{24,16},{28,... | collective-permute-start | bytes 786440 | tf_op jit(solution)/shard_map/ppermute | solution.py:21
  180.7 13.6 %collective-permute-start.9 = (bf16[256,512]{0,1:T(8,128)(2,1)S(1)}, bf16[256,512]{0,1:T(8,128)(2,1)S(1)}, u32[]{:S(2)}, u32[]{:S(2)}) collective-permute-start(bf16[256,512]{0,1:T(8,128)(2,1)S(1)} %get-tuple-element.22), channel_id=1, source_target_pairs={{12,0},{13,1},{14,2},{15,3},{28,16},{29,17},{30,18},{31,19}} | collective-permute-start | bytes 786440 | tf_op jit(solution)/shard_map/ppermute | solution.py:21
  183.1 5.1 %copy-start.2 = (bf16[256,4,128]{2,1,0:T(4,128)(2,1)}, bf16[256,4,128]{2,1,0:T(4,128)(2,1)S(1)}, u32[]{:S(2)}) copy-start(bf16[256,4,128]{2,1,0:T(4,128)(2,1)S(1)} %fusion.20) | copy-start | bytes 786436
  183.1 11.3 %copy-start.9 = (f32[2,128,1024,1]{2,1,3,0:T(8,128)S(1)}, f32[2,128,1024,1]{2,1,3,0:T(8,128)}, u32[]{:S(2)}) copy-start(f32[2,128,1024,1]{2,1,3,0:T(8,128)} %fusion.80) | copy-start | bytes 3145732
  183.1 11.2 %copy-start.15 = (f32[2,128,1024,1]{2,1,3,0:T(8,128)S(1)}, f32[2,128,1024,1]{2,1,3,0:T(8,128)}, u32[]{:S(2)}) copy-start(f32[2,128,1024,1]{2,1,3,0:T(8,128)} %fusion.14) | copy-start | bytes 3145732
  184.7 31.4 %collective-permute-start.12 = (bf16[1344,512]{1,0:T(8,128)(2,1)}, bf16[1344,512]{1,0:T(8,128)(2,1)}, u32[]{:S(2)}, u32[]{:S(2)}) collective-permute-start(bf16[1344,512]{1,0:T(8,128)(2,1)} %convolution_convert_fusion.5), channel_id=1, source_target_pairs={{0,4},{4,0},{8,12},{12,8},{1,5},{5,1},{9,13},{13,9},{2,6},{6,2},{1... | collective-permute-start | bytes 4128776 | tf_op jit(solution)/shard_map/ppermute | solution.py:26
  196.0 2.6 copy-start.35
  198.6 20.6 %collective-permute-start.13 = (bf16[512,1344]{0,1:T(8,128)(2,1)}, bf16[512,1344]{0,1:T(8,128)(2,1)}, u32[]{:S(2)}, u32[]{:S(2)}) collective-permute-start(bf16[512,1344]{0,1:T(8,128)(2,1)} %convolution_convert_fusion.4), channel_id=1, source_target_pairs={{0,4},{4,0},{8,12},{12,8},{1,5},{5,1},{9,13},{13,9},{2,6},{6,2},{1... | collective-permute-start | bytes 4128776 | tf_op jit(solution)/shard_map/ppermute | solution.py:26
  216.0 14.5 %copy-start.5 = (bf16[256,512]{0,1:T(8,128)(2,1)}, bf16[256,512]{0,1:T(8,128)(2,1)S(1)}, u32[]{:S(2)}) copy-start(bf16[256,512]{0,1:T(8,128)(2,1)S(1)} %pad_maximum_fusion.3) | copy-start | bytes 786436
  222.2 1.9 copy-start.10
  230.6 1.9 copy-start.3
  240.9 2.2 copy-start.4
  240.9 5.9 %slice-start = ((s8[5505024]{0:T(1024)(128)(4,1)}), s8[4194304]{0:T(1024)(128)(4,1)S(1)}, s32[]{:S(2)}) async-start(s8[5505024]{0:T(1024)(128)(4,1)} %bitcast.120), calls=%async_computation.7 | async-start | bytes 8388608
  242.6 2.4 copy-start.6
  242.6 10.5 %collective-permute-start.14 = (bf16[1344,512]{1,0:T(8,128)(2,1)S(1)}, bf16[1344,512]{1,0:T(8,128)(2,1)S(1)}, u32[]{:S(2)}, u32[]{:S(2)}) collective-permute-start(bf16[1344,512]{1,0:T(8,128)(2,1)S(1)} %convolution_convert_fusion.3), channel_id=1, source_target_pairs={{0,4},{4,0},{8,12},{12,8},{1,5},{5,1},{9,13},{13,9},{2,6},{6,2},{1... | collective-permute-start | bytes 4128776 | tf_op jit(solution)/shard_map/ppermute | solution.py:26
  243.8 3.1 slice-start.1
  244.4 37.6 %collective-permute-start.19 = (bf16[512,1344]{0,1:T(8,128)(2,1)S(1)}, bf16[512,1344]{0,1:T(8,128)(2,1)S(1)}, u32[]{:S(2)}, u32[]{:S(2)}) collective-permute-start(bf16[512,1344]{0,1:T(8,128)(2,1)S(1)} %convolution_convert_fusion), channel_id=1, source_target_pairs={{0,4},{4,0},{8,12},{12,8},{1,5},{5,1},{9,13},{13,9},{2,6},{6,2},{1... | collective-permute-start | bytes 4128776 | tf_op jit(solution)/shard_map/ppermute | solution.py:26
  245.5 1.3 copy-start.24
  245.5 7.0 %collective-permute-start.17 = (bf16[1344,512]{1,0:T(8,128)(2,1)S(1)}, bf16[1344,512]{1,0:T(8,128)(2,1)S(1)}, u32[]{:S(2)}, u32[]{:S(2)}) collective-permute-start(bf16[1344,512]{1,0:T(8,128)(2,1)S(1)} %convolution_convert_fusion.1), channel_id=1, source_target_pairs={{0,4},{4,0},{8,12},{12,8},{1,5},{5,1},{9,13},{13,9},{2,6},{6,2},{1... | collective-permute-start | bytes 4128776 | tf_op jit(solution)/shard_map/ppermute | solution.py:26
  246.8 2.5 copy-start.23
  246.8 33.0 %collective-permute-start.15 = (bf16[1344,512]{1,0:T(8,128)(2,1)S(1)}, bf16[1344,512]{1,0:T(8,128)(2,1)S(1)}, u32[]{:S(2)}, u32[]{:S(2)}) collective-permute-start(bf16[1344,512]{1,0:T(8,128)(2,1)S(1)} %copy-done.24), channel_id=1, source_target_pairs={{0,8},{4,12},{8,0},{12,4},{1,9},{5,13},{9,1},{13,5},{2,10},{6,14},... | collective-permute-start | bytes 4128776 | tf_op jit(solution)/shard_map/ppermute | solution.py:26
  249.4 60.0 %collective-permute-start.20 = (bf16[512,1344]{0,1:T(8,128)(2,1)S(1)}, bf16[512,1344]{0,1:T(8,128)(2,1)S(1)}, u32[]{:S(2)}, u32[]{:S(2)}) collective-permute-start(bf16[512,1344]{0,1:T(8,128)(2,1)S(1)} %copy-done.23), channel_id=1, source_target_pairs={{0,8},{4,12},{8,0},{12,4},{1,9},{5,13},{9,1},{13,5},{2,10},{6,14},... | collective-permute-start | bytes 4128776 | tf_op jit(solution)/shard_map/ppermute | solution.py:26
  252.5 59.0 %collective-permute-start.16 = (bf16[1344,512]{1,0:T(8,128)(2,1)S(1)}, bf16[1344,512]{1,0:T(8,128)(2,1)S(1)}, u32[]{:S(2)}, u32[]{:S(2)}) collective-permute-start(bf16[1344,512]{1,0:T(8,128)(2,1)S(1)} %convolution_convert_fusion.2), channel_id=1, source_target_pairs={{0,4},{4,0},{8,12},{12,8},{1,5},{5,1},{9,13},{13,9},{2,6},{6,2},{1... | collective-permute-start | bytes 4128776 | tf_op jit(solution)/shard_map/ppermute | solution.py:26
  253.1 84.8 %collective-permute-start.18 = (bf16[1344,512]{1,0:T(8,128)(2,1)S(1)}, bf16[1344,512]{1,0:T(8,128)(2,1)S(1)}, u32[]{:S(2)}, u32[]{:S(2)}) collective-permute-start(bf16[1344,512]{1,0:T(8,128)(2,1)S(1)} %add_convert_fusion), channel_id=1, source_target_pairs={{0,8},{4,12},{8,0},{12,4},{1,9},{5,13},{9,1},{13,5},{2,10},{6,14},... | collective-permute-start | bytes 4128776 | tf_op jit(solution)/shard_map/ppermute | solution.py:26
  (8 other events, 7.3 us)
Sparse Core Ops, SparseCore 0:
  9.6 59.6 all-gather.3
  70.9 44.5 all-gather.5
  122.7 29.3 reduce-scatter.2
  164.8 26.5 all-gather.7
  241.0 51.9 reduce-scatter.4
where the time goes:
time: 349 us; the launch traced here: 347 us
  waiting for transfers between devices  154 us (44%)
  matrix products  74.8 us (21%)
  local copies, waits for them, and re-layouts  49.1 us (14%)
  other arithmetic  34.3 us (10%)
  starting transfers between devices  20.3 us (6%)
  between operations  14.6 us (4%)
    ppermute x15, waiting for transfers between devices, swapped(): lax.ppermute(value, axis, [(source, source ^ bit) for source in range(cou...  137 us
    dot_general x8, matrix products, project(): total = total + jnp.dot(columns, piece, preferred_element_type=jnp.float32)  17.5 us
    dot_general x12, matrix products, product(): jnp.einsum('td,tc->dc', picked, right, preferred_element_type=jnp.float32)  15.8 us
    unnamed x98, local copies, waits for them, and re-layouts  15.1 us
    ppermute x6, starting transfers between devices, shifted(): lax.ppermute(value, axis, [(source, source + steps) for source in range(f...  12.4 us
    dot_general x4, matrix products, local(): jnp.einsum('tc,dc->td', query_back, query_pieces[offset], preferred_eleme...  11.4 us
    reduce_scatter x1, waiting for transfers between devices, local(): lax.psum_scatter(partial_heads.astype(jnp.bfloat16), 'hid', scatter_dimen...  9.2 us
    dot_general x4, matrix products, local(): jnp.einsum('tc,dc->td', kv_back, kv_pieces[offset], preferred_element_typ...  8.33 us
  transfers between devices with their start and end apart: 26, of which 8 were waited for; matrix products, arithmetic and copies ran while one was open for 34% of the time, Pallas kernels for 0%

commit v1 on v0

--- a/solution.py
+++ b/solution.py
@@ -55,18 +55,24 @@
     return totals
 
 
-def finish_scatter(totals, axis):
+def exchange_far(totals, axis):
     count = lax.axis_size(axis)
     totals = dict(totals)
     bit = 2
     while bit < count:
         for offset in range(count - bit, 0, -2 * bit):
-            arrived = swapped(totals[offset], axis, bit).astype(jnp.float32)
+            arrived = swapped(totals[offset], axis, bit)
             kept = offset ^ bit
-            total = totals[kept].astype(jnp.float32) + arrived
+            if kept == 0 and 2 * bit == count:
+                return totals[0], arrived
+            total = totals[kept].astype(jnp.float32) + arrived.astype(jnp.float32)
             totals[kept] = total.astype(jnp.bfloat16) if kept else total
         bit *= 2
-    return totals[0]
+    return totals[0], jnp.zeros_like(totals[0], jnp.bfloat16)
+
+
+def finish(pair):
+    return pair[0] + pair[1].astype(jnp.float32)
 
 
 def ordered(value, *groups):
@@ -135,9 +141,8 @@
     key_unnormed = kv_unnormed[:, :kv_cols]
     value_raw = kv_unnormed[:, kv_cols:]
     partial_heads = jnp.einsum("td,hd->th", grad_out, full_wo, preferred_element_type=jnp.float32)
-    attended_gradient = lax.psum_scatter(
-        partial_heads.astype(jnp.bfloat16), "hid", scatter_dimension=1, tiled=True
-    )
+    partial_heads = partial_heads.astype(jnp.bfloat16)
+    attended_gradient = lax.psum_scatter(partial_heads, "hid", scatter_dimension=1, tiled=True)
     values_local = value_raw.astype(jnp.bfloat16)
     token_pos = lax.dynamic_slice_in_dim(positions, first_token, TOK_DEV, 0)
     cosine_table, sine_table = rotary_tables(token_pos)
@@ -222,6 +227,8 @@
         .astype(jnp.bfloat16)
         .reshape(TOK_DEV, query_cols)
     )
+    query_sums = begin_scatter(full_rows, query_back, "tok")
+    grad_kv, (query_sums,) = ordered(grad_kv, query_sums)
     key_backward = (
         key_pullback(grad_kv[:, :kv_cols].reshape(TOK_DEV, key_value_heads, HEAD_SIZE))[0]
         .astype(jnp.bfloat16)
@@ -229,23 +236,27 @@
     )
     value_backward = grad_kv[:, kv_cols:].astype(jnp.bfloat16)
     kv_back = jnp.concatenate([key_backward, value_backward], 1)
-    query_sums = begin_scatter(full_rows, query_back, "tok")
     out_sums = begin_scatter(all_heads, grad_out, "tok")
-    kv_back, (query_sums, out_sums) = ordered(kv_back, query_sums, out_sums)
+    kv_back, (out_sums,) = ordered(kv_back, out_sums)
+    query_near, query_far = exchange_far(query_sums, "tok")
+    out_near, out_far = exchange_far(out_sums, "tok")
+    kv_later, query_far = lax.optimization_barrier((kv_back, query_far))
+    kv_last, out_far = lax.optimization_barrier((kv_back, out_far))
     block_rows = jnp.zeros((TOK_DEV, full_rows.shape[1]), jnp.bfloat16)
     for offset in range(len(query_pieces)):
+        kv_used = kv_back if 2 * offset < len(query_pieces) else kv_later
         product = jnp.einsum(
             "tc,dc->td", query_back, query_pieces[offset], preferred_element_type=jnp.float32
-        ) + jnp.einsum("tc,dc->td", kv_back, kv_pieces[offset], preferred_element_type=jnp.float32)
+        ) + jnp.einsum("tc,dc->td", kv_used, kv_pieces[offset], preferred_element_type=jnp.float32)
         start = (block_index ^ offset) * height
         block_rows = lax.dynamic_update_slice_in_dim(
             block_rows, product.astype(jnp.bfloat16), start, 1
         )
     grad_x = lax.psum_scatter(block_rows, "hid", scatter_dimension=1, tiled=True)
-    kv_sums = begin_scatter(full_rows, kv_back, "tok")
-    grad_wq = finish_scatter(query_sums, "tok")
-    grad_wo = finish_scatter(out_sums, "tok")
-    grad_wkv = finish_scatter(kv_sums, "tok")
+    kv_sums = begin_scatter(full_rows, kv_last, "tok")
+    grad_wq = finish((query_near, query_far))
+    grad_wo = finish((out_near, out_far))
+    grad_wkv = finish(exchange_far(kv_sums, "tok"))
     key_weight_gradient = grad_wkv[:, :kv_cols]
     value_weight_gradient = grad_wkv[:, kv_cols:]
     return (attn_out, grad_x, grad_wq, key_weight_gradient, value_weight_gradient, grad_wo)

time: 349 us -> 323 us (0.926)
  waiting for transfers between devices: 154 us -> 126 us
  other arithmetic: 34.3 us -> 40.4 us
  local copies, waits for them, and re-layouts: 49.1 us -> 45.2 us
    ppermute x15, waiting for transfers between devices: 137 us -> 106 us  [swapped(): lax.ppermute(value, axis, [(source, source ^ bit) for source in range(cou...]
    unnamed x98 -> x82, local copies, waits for them, and re-layouts: 15.1 us -> 13.7 us
  transfers between devices with their start and end apart: 26 -> 26, of which waited for: 8 -> 8; matrix products, arithmetic and copies ran while one was open for 34% -> 46% of each run, Pallas kernels for 0% -> 0%
where the time goes in v1:
time: 323 us; the launch traced here: 321 us
  waiting for transfers between devices  126 us (39%)
  matrix products  77.3 us (24%)
  local copies, waits for them, and re-layouts  45.2 us (14%)
  other arithmetic  40.4 us (13%)
  starting transfers between devices  18.1 us (6%)
  between operations  14.5 us (4%)
    ppermute x15, waiting for transfers between devices, swapped(): lax.ppermute(value, axis, [(source, source ^ bit) for source in range(cou...  106 us
    dot_general x8, matrix products, project(): total = total + jnp.dot(columns, piece, preferred_element_type=jnp.float32)  17.5 us
    dot_general x12, matrix products, product(): jnp.einsum('td,tc->dc', picked, right, preferred_element_type=jnp.float32)  15.8 us
    unnamed x82, local copies, waits for them, and re-layouts  13.7 us
    ppermute x6, starting transfers between devices, shifted(): lax.ppermute(value, axis, [(source, source + steps) for source in range(f...  12.7 us
    dot_general x4, matrix products, local(): jnp.einsum('tc,dc->td', query_back, query_pieces[offset], preferred_eleme...  11.3 us
    ppermute x6, waiting for transfers between devices, shifted(): lax.ppermute(value, axis, [(source, source + steps) for source in range(f...  9.37 us
    reduce_scatter x1, waiting for transfers between devices, local(): lax.psum_scatter(partial_heads, 'hid', scatter_dimension=1, tiled=True)  9.2 us
  transfers between devices with their start and end apart: 26, of which 8 were waited for; matrix products, arithmetic and copies ran while one was open for 46% of the time, Pallas kernels for 0%

profile of v1, /device:TPU:0, one launch (start us, length us, event | category | flops | bytes accessed | tf_op | source)
XLA Modules:
  0.0 321.4 jit_solution(11473392351920477866)
XLA Ops:
  10.5 3.0 collective-permute-start.1
  14.2 30.6 %collective-permute-done.1 = bf16[1344,512]{1,0:T(8,128)(2,1)} collective-permute-done((bf16[1344,512]{1,0:T(8,128)(2,1)}, bf16[1344,512]{1,0:T(8,128)(2,1)}, u32[]{:S(2)}, u32[]{:S(2)}) %collective-permute-start.1) | collective-permute-done | bytes 1376288 | tf_op jit(solution)/shard_map/ppermute | solution.py:26
  46.1 1.5 fusion.19
  47.6 25.8 %collective-permute-done.7 = bf16[1344,512]{1,0:T(8,128)(2,1)} collective-permute-done((bf16[1344,512]{1,0:T(8,128)(2,1)}, bf16[1344,512]{1,0:T(8,128)(2,1)}, u32[]{:S(2)}, u32[]{:S(2)}) %collective-permute-start.7) | collective-permute-done | bytes 1376288 | tf_op jit(solution)/shard_map/ppermute | solution.py:26
  73.5 2.1 fusion.50
  75.7 2.5 convolution_add_fusion.11
  78.6 2.3 convolution_add_fusion.10
  81.0 1.9 convolution_add_fusion.9
  84.4 1.8 reshape.229
  86.2 2.0 multiply_reduce_fusion.3
  94.9 3.0 collective-permute-start.5
  97.9 3.6 %collective-permute-start.4 = (bf16[256,512]{1,0:T(8,128)(2,1)}, bf16[256,512]{1,0:T(8,128)(2,1)}, u32[]{:S(2)}, u32[]{:S(2)}) collective-permute-start(bf16[256,512]{1,0:T(8,128)(2,1)} %pad_maximum_fusion.1), channel_id=1, source_target_pairs={{0,8},{4,12},{1,9},{5,13},{2,10},{6,14},{3,11},{7,15},{16,24},{20,... | collective-permute-start | bytes 786440 | tf_op jit(solution)/shard_map/ppermute | solution.py:21
  101.5 2.0 collective-permute-start.3
  103.5 1.9 fusion.48
  105.4 1.9 convolution_add_fusion.8
  107.4 1.9 convolution_add_fusion.7
  109.3 2.7 convolution_add_fusion.6
  112.1 2.0 reshape.232
  114.1 2.0 multiply_reduce_fusion.1
  117.1 5.3 %convolution_convert_fusion.7 = bf16[256,2048]{1,0:T(8,128)(2,1)} fusion(bf16[256,1344]{0,1:T(8,128)(2,1)S(1)} %copy-done, bf16[2048,1344]{0,1:T(8,128)(2,1)} %all-gather.6.cloned.1.call-done), kind=kOutput, calls=%fused_computation.35 | convolution fusion | flops 1409810432 | bytes 7241728 | tf_op jit(solution)/shard_map/td,hd->th/dot_general | solution.py:143
  130.2 2.0 reshape.230
  132.2 2.0 reshape.231
  134.2 2.0 copy.82
  136.2 2.7 fusion.4
  138.9 2.0 copy-done.15
  141.0 1.9 convolution_convert_fusion.8
  142.9 9.2 %reduce-scatter.3.cloned.1.call-done = bf16[256,512]{1,0:T(8,128)(2,1)} async-done(((bf16[256,2048]{1,0:T(8,128)(2,1)}), bf16[256,512]{1,0:T(8,128)(2,1)}) %reduce-scatter.3.cloned.1.call-update) | async-done | bytes 262160 | tf_op jit(solution)/shard_map/reduce_scatter | solution.py:145
  152.1 1.8 copy.103
  153.9 5.9 %fusion = (f32[2,2,256]{2,1,0:T(2,128)S(1)}, f32[2,1024,256,2]{2,1,3,0:T(8,128)}) fusion(f32[2,2,256]{2,1,0:T(2,128)S(1)} %get-tuple-element.49, f32[2,1024,256,2]{2,1,3,0:T(8,128)} %copy-done.15, pred[256,1024]{0,1:T(8,128)(4,1)} %fusion.19, bf16[256,2,2,128]{0,3,2,1:T(8,128)(2,1)} %bitcast.138, bf16[1024,2,128,1]{2,1,0,3:T(2,128)(2,1)} %bitcast.134), kind=kOutput, calls=%fused_computation.2 | convolution fusion | flops 273677312 | bytes 9445376 | tf_op jit(solution)/shard_map/tkgd,ukd->kgtu/dot_general | solution.py:191
  159.7 2.3 fusion.16
  162.1 4.7 %fusion.2 = bf16[2,2,256,1024]{2,3,1,0:T(8,128)(2,1)S(1)} fusion(f32[2,1024,256,2]{2,1,3,0:T(8,128)} %get-tuple-element.52, f32[2,2,256]{2,1,0:T(2,128)S(1)} %get-tuple-element.51, f32[2,2,256]{2,1,0:T(2,128)S(1)} %get-tuple-element.49, f32[2,1024,256,2]{2,1,3,0:T(8,128)} %copy-done.15, pred[256,1024]{0,1:T(8,128)(4,1)} %fusion.19), kind=kLoop, calls=%fused_computation.4 | loop fusion | flops 7340032 | bytes 10756096 | tf_op jit(solution)/shard_map/convert_element_type | solution.py:199
  168.3 2.0 copy.100
  170.3 1.9 copy.99
  172.3 1.6 multiply_add_fusion.1
  178.0 2.3 fusion.22
  180.3 1.6 convolution_convert_fusion.5
  186.0 1.5 collective-permute-start.9
  187.5 3.0 fusion.60
  190.5 7.6 %collective-permute-done.10 = bf16[256,512]{0,1:T(8,128)(2,1)S(1)} collective-permute-done((bf16[256,512]{0,1:T(8,128)(2,1)S(1)}, bf16[256,512]{0,1:T(8,128)(2,1)S(1)}, u32[]{:S(2)}, u32[]{:S(2)}) %collective-permute-start.10) | collective-permute-done | bytes 262176 | tf_op jit(solution)/shard_map/ppermute | solution.py:21
  198.1 1.7 collective-permute-done.9
  200.8 2.6 convolution_convert_fusion.4
  203.4 3.0 add_convert_fusion.1
  207.8 1.7 copy.102
  209.6 1.7 copy.101
  213.5 2.2 multiply_reduce_fusion.2
  217.6 2.7 fusion.52
  220.3 1.7 copy.98
  223.0 3.1 add_convert_fusion
  226.1 13.2 %collective-permute-done.14 = bf16[1344,512]{1,0:T(8,128)(2,1)} collective-permute-done((bf16[1344,512]{1,0:T(8,128)(2,1)}, bf16[1344,512]{1,0:T(8,128)(2,1)}, u32[]{:S(2)}, u32[]{:S(2)}) %collective-permute-start.14) | collective-permute-done | bytes 1376288 | tf_op jit(solution)/shard_map/ppermute | solution.py:26
  239.6 1.7 broadcast_in_dim.16
  241.3 2.7 fusion.14
  244.0 1.9 fusion.113
  245.9 1.9 fusion.114
  247.8 2.7 fusion.8
  250.5 2.8 fusion.10
  253.4 1.9 fusion.115
  255.2 2.8 fusion.12
  258.1 1.5 convolution_convert_fusion.3
  260.3 11.1 %collective-permute-done.16 = bf16[512,1344]{0,1:T(8,128)(2,1)} collective-permute-done((bf16[512,1344]{0,1:T(8,128)(2,1)}, bf16[512,1344]{0,1:T(8,128)(2,1)}, u32[]{:S(2)}, u32[]{:S(2)}) %collective-permute-start.16) | collective-permute-done | bytes 1376288 | tf_op jit(solution)/shard_map/ppermute | solution.py:26
  273.1 5.1 %convolution_convert_fusion.6 = bf16[256,1344]{0,1:T(8,128)(2,1)} fusion(bf16[2048,1344]{0,1:T(8,128)(2,1)} %all-gather.6.cloned.1.call-done, bf16[256,2048]{0,1:T(8,128)(2,1)S(1)} %copy-done.28), kind=kOutput, calls=%fused_computation.34 | convolution fusion | flops 1409630208 | bytes 7241728 | tf_op jit(solution)/shard_map/dot_general | solution.py:188
  280.5 3.4 %convert_add_fusion.1 = f32[1344,512]{1,0:T(8,128)} fusion(bf16[1344,512]{1,0:T(8,128)(2,1)} %collective-permute-done.14, f32[1344,512]{1,0:T(8,128)S(1)} %fusion.46, bf16[1344,512]{1,0:T(8,128)(2,1)S(1)} %collective-permute-done.15), kind=kLoop, calls=%fused_computation.23 | loop fusion | flops 2752512 | bytes 8257536 | tf_op jit(solution)/shard_map/add | solution.py:75
  283.9 3.4 %convert_add_fusion = f32[512,1344]{0,1:T(8,128)} fusion(bf16[512,1344]{0,1:T(8,128)(2,1)} %collective-permute-done.16, f32[512,1344]{0,1:T(8,128)S(1)} %fusion.63, bf16[512,1344]{0,1:T(8,128)(2,1)S(1)} %collective-permute-done.20), kind=kLoop, calls=%fused_computation.22 | loop fusion | flops 2752512 | bytes 8257536 | tf_op jit(solution)/shard_map/add | solution.py:75
  287.4 25.2 %collective-permute-done.19 = bf16[1344,512]{1,0:T(8,128)(2,1)S(1)} collective-permute-done((bf16[1344,512]{1,0:T(8,128)(2,1)S(1)}, bf16[1344,512]{1,0:T(8,128)(2,1)S(1)}, u32[]{:S(2)}, u32[]{:S(2)}) %collective-permute-start.19) | collective-permute-done | bytes 1376288 | tf_op jit(solution)/shard_map/ppermute | solution.py:26
  313.1 1.7 fusion.107
  (171 shorter events, 45.0 us)
Async XLA Ops:
  7.2 109.9 %copy-start = (bf16[256,1344]{0,1:T(8,128)(2,1)S(1)}, bf16[256,1344]{0,1:T(8,128)(2,1)}, u32[]{:S(2)}) copy-start(bf16[256,1344]{0,1:T(8,128)(2,1)} %param.17) | copy-start | bytes 2064388
  7.2 1.6 copy-start.31
  7.2 2.5 copy-start.32
  7.2 66.3 %all-gather.4.cloned.1.call-start = ((), (), s32[]{:S(2)}) async-start(), calls=%async_computation.2 | async-start | bytes 3440640 | tf_op jit(solution)/shard_map/all_gather | solution.py:125
  7.9 6.1 %copy-start.35 = (s32[1024]{0:T(1024)S(1)}, s32[1024]{0:T(1024)}, u32[]{:S(2)}) copy-start(s32[1024]{0:T(1024)} %param.16) | copy-start | bytes 12292
  7.9 109.2 %all-gather.6.cloned.1.call-start = ((), (), s32[]{:S(2)}) async-start(), calls=%async_computation.3 | async-start | bytes 6881280 | tf_op jit(solution)/shard_map/all_gather | solution.py:128
  8.7 143.4 %reduce-scatter.3.cloned.1.call-start = ((), (), s32[]{:S(2)}) async-start(), calls=%async_computation.4 | async-start | bytes 1310720 | tf_op jit(solution)/shard_map/reduce_scatter | solution.py:145
  10.5 34.3 %collective-permute-start.1 = (bf16[1344,512]{1,0:T(8,128)(2,1)}, bf16[1344,512]{1,0:T(8,128)(2,1)}, u32[]{:S(2)}, u32[]{:S(2)}) collective-permute-start(bf16[1344,512]{1,0:T(8,128)(2,1)} %constant_dynamic-update-slice_fusion), channel_id=1, source_target_pairs={{0,8},{4,12},{8,0},{12,4},{1,9},{5,13},{9,1},{13,5},{2,10},{6,14},... | collective-permute-start | bytes 4128776 | tf_op jit(solution)/shard_map/ppermute | solution.py:26
  13.5 60.0 %collective-permute-start.7 = (bf16[1344,512]{1,0:T(8,128)(2,1)}, bf16[1344,512]{1,0:T(8,128)(2,1)}, u32[]{:S(2)}, u32[]{:S(2)}) collective-permute-start(bf16[1344,512]{1,0:T(8,128)(2,1)} %param.10), channel_id=1, source_target_pairs={{0,8},{4,12},{8,0},{12,4},{1,9},{5,13},{9,1},{13,5},{2,10},{6,14},... | collective-permute-start | bytes 4128776 | tf_op jit(solution)/shard_map/ppermute | solution.py:26
  13.5 62.1 %collective-permute-start = (bf16[1344,512]{1,0:T(8,128)(2,1)}, bf16[1344,512]{1,0:T(8,128)(2,1)}, u32[]{:S(2)}, u32[]{:S(2)}) collective-permute-start(bf16[1344,512]{1,0:T(8,128)(2,1)} %constant_dynamic-update-slice_fusion), channel_id=1, source_target_pairs={{0,4},{4,0},{8,12},{12,8},{1,5},{5,1},{9,13},{13,9},{2,6},{6,2},{1... | collective-permute-start | bytes 4128776 | tf_op jit(solution)/shard_map/ppermute | solution.py:26
  13.5 91.9 %collective-permute-start.6 = (bf16[1344,512]{1,0:T(8,128)(2,1)}, bf16[1344,512]{1,0:T(8,128)(2,1)}, u32[]{:S(2)}, u32[]{:S(2)}) collective-permute-start(bf16[1344,512]{1,0:T(8,128)(2,1)} %param.10), channel_id=1, source_target_pairs={{0,4},{4,0},{8,12},{12,8},{1,5},{5,1},{9,13},{13,9},{2,6},{6,2},{1... | collective-permute-start | bytes 4128776 | tf_op jit(solution)/shard_map/ppermute | solution.py:26
  44.8 36.1 %collective-permute-start.2 = (bf16[1344,512]{1,0:T(8,128)(2,1)}, bf16[1344,512]{1,0:T(8,128)(2,1)}, u32[]{:S(2)}, u32[]{:S(2)}) collective-permute-start(bf16[1344,512]{1,0:T(8,128)(2,1)} %collective-permute-done.1), channel_id=1, source_target_pairs={{0,4},{4,0},{8,12},{12,8},{1,5},{5,1},{9,13},{13,9},{2,6},{6,2},{1... | collective-permute-start | bytes 4128776 | tf_op jit(solution)/shard_map/ppermute | solution.py:26
  73.5 35.8 %collective-permute-start.8 = (bf16[1344,512]{1,0:T(8,128)(2,1)}, bf16[1344,512]{1,0:T(8,128)(2,1)}, u32[]{:S(2)}, u32[]{:S(2)}) collective-permute-start(bf16[1344,512]{1,0:T(8,128)(2,1)} %collective-permute-done.7), channel_id=1, source_target_pairs={{0,4},{4,0},{8,12},{12,8},{1,5},{5,1},{9,13},{13,9},{2,6},{6,2},{1... | collective-permute-start | bytes 4128776 | tf_op jit(solution)/shard_map/ppermute | solution.py:26
  75.6 3.0 copy-start.1
  81.0 9.0 %copy-start.37 = (f32[128]{0:T(128)S(1)}, f32[128]{0:T(128)}, u32[]{:S(2)}) copy-start(f32[128]{0:T(128)} %param.15) | copy-start | bytes 1540
  82.9 0.8 copy-start.20
  92.3 13.2 %copy-start.22 = (bf16[256,256]{1,0:T(8,128)(2,1)}, bf16[256,256]{1,0:T(8,128)(2,1)S(1)}, u32[]{:S(2)}) copy-start(bf16[256,256]{1,0:T(8,128)(2,1)S(1)} %slice.108) | copy-start | bytes 393220
  94.2 7.3 %copy-start.24 = (bf16[32,8,2,128]{3,1,2,0:T(8,128)(2,1)}, bf16[32,8,2,128]{3,1,2,0:T(8,128)(2,1)S(1)}, u32[]{:S(2)}) copy-start(bf16[32,8,2,128]{3,1,2,0:T(8,128)(2,1)S(1)} %copy.145) | copy-start | bytes 393220
  94.9 33.0 %collective-permute-start.5 = (bf16[256,512]{1,0:T(8,128)(2,1)}, bf16[256,512]{1,0:T(8,128)(2,1)}, u32[]{:S(2)}, u32[]{:S(2)}) collective-permute-start(bf16[256,512]{1,0:T(8,128)(2,1)} %pad_maximum_fusion.1), channel_id=1, source_target_pairs={{0,4},{4,8},{8,12},{1,5},{5,9},{9,13},{2,6},{6,10},{10,14},{3,7},{... | collective-permute-start | bytes 786440 | tf_op jit(solution)/shard_map/ppermute | solution.py:21
  97.9 30.1 %collective-permute-start.4 = (bf16[256,512]{1,0:T(8,128)(2,1)}, bf16[256,512]{1,0:T(8,128)(2,1)}, u32[]{:S(2)}, u32[]{:S(2)}) collective-permute-start(bf16[256,512]{1,0:T(8,128)(2,1)} %pad_maximum_fusion.1), channel_id=1, source_target_pairs={{0,8},{4,12},{1,9},{5,13},{2,10},{6,14},{3,11},{7,15},{16,24},{20,... | collective-permute-start | bytes 786440 | tf_op jit(solution)/shard_map/ppermute | solution.py:21
  101.5 26.5 %collective-permute-start.3 = (bf16[256,512]{1,0:T(8,128)(2,1)}, bf16[256,512]{1,0:T(8,128)(2,1)}, u32[]{:S(2)}, u32[]{:S(2)}) collective-permute-start(bf16[256,512]{1,0:T(8,128)(2,1)} %pad_maximum_fusion.1), channel_id=1, source_target_pairs={{0,12},{1,13},{2,14},{3,15},{16,28},{17,29},{18,30},{19,31}} | collective-permute-start | bytes 786440 | tf_op jit(solution)/shard_map/ppermute | solution.py:21
  117.1 6.4 %copy-start.36 = (f32[128]{0:T(128)S(1)}, f32[128]{0:T(128)}, u32[]{:S(2)}) copy-start(f32[128]{0:T(128)} %param.14) | copy-start | bytes 1540
  122.5 78.3 %all-gather.8.cloned.1.call-start = ((), (), s32[]{:S(2)}) async-start(), calls=%async_computation.5 | async-start | bytes 1310720 | tf_op jit(solution)/shard_map/all_gather | solution.py:187
  123.6 4.4 %copy-start.23 = (bf16[256,256]{1,0:T(8,128)(2,1)S(1)}, bf16[256,256]{1,0:T(8,128)(2,1)}, u32[]{:S(2)}) copy-start(bf16[256,256]{1,0:T(8,128)(2,1)} %copy-done.22) | copy-start | bytes 393220
  123.6 4.4 %copy-start.25 = (bf16[32,8,2,128]{3,1,2,0:T(8,128)(2,1)S(1)}, bf16[32,8,2,128]{3,1,2,0:T(8,128)(2,1)}, u32[]{:S(2)}) copy-start(bf16[32,8,2,128]{3,1,2,0:T(8,128)(2,1)} %copy-done.24) | copy-start | bytes 393220
  136.2 4.7 %copy-start.29 = (pred[256,1024]{0,1:T(8,128)(4,1)S(1)}, pred[256,1024]{0,1:T(8,128)(4,1)}, u32[]{:S(2)}) copy-start(pred[256,1024]{0,1:T(8,128)(4,1)} %fusion.19) | copy-start | bytes 786436
  136.2 4.7 %copy-start.33 = (bf16[1024,2,128]{2,1,0:T(2,128)(2,1)S(1)}, bf16[1024,2,128]{2,1,0:T(2,128)(2,1)}, u32[]{:S(2)}) copy-start(bf16[1024,2,128]{2,1,0:T(2,128)(2,1)} %reshape.230) | copy-start | bytes 1572868
  138.9 2.1 copy-start.15
  153.9 5.9 %copy-start.16 = (f32[2,1024,256,2]{2,1,3,0:T(8,128)S(1)}, f32[2,1024,256,2]{2,1,3,0:T(8,128)}, u32[]{:S(2)}) copy-start(f32[2,1024,256,2]{2,1,3,0:T(8,128)} %copy-done.15) | copy-start | bytes 12582916
  153.9 5.9 %copy-start.30 = (pred[256,1024]{0,1:T(8,128)(4,1)S(1)}, pred[256,1024]{0,1:T(8,128)(4,1)}, u32[]{:S(2)}) copy-start(pred[256,1024]{0,1:T(8,128)(4,1)} %fusion.19) | copy-start | bytes 786436
  153.9 5.9 %copy-start.34 = (bf16[256,512]{0,1:T(8,128)(2,1)S(1)}, bf16[256,512]{0,1:T(8,128)(2,1)}, u32[]{:S(2)}) copy-start(bf16[256,512]{0,1:T(8,128)(2,1)} %copy.103) | copy-start | bytes 786436
  162.0 152.8 %reduce-scatter.5.cloned.1.call-start = ((), (), s32[]{:S(2)}) async-start(), calls=%async_computation.6 | async-start | bytes 3440640 | tf_op jit(solution)/shard_map/reduce_scatter | solution.py:255
  162.1 4.8 %copy-start.19 = (bf16[1024,2,128,1]{0,2,3,1:T(8,128)(2,1)S(1)}, bf16[1024,2,128,1]{0,2,3,1:T(8,128)(2,1)}, u32[]{:S(2)}) copy-start(bf16[1024,2,128,1]{0,2,3,1:T(8,128)(2,1)} %copy.82) | copy-start | bytes 1572868
  166.9 1.5 copy-start.8
  172.3 2.6 copy-start.10
  173.9 0.8 copy-start.12
  173.9 1.0 copy-start.13
  178.0 4.0 %copy-start.9 = (bf16[2,2,256,1024]{2,3,1,0:T(8,128)(2,1)S(1)}, bf16[2,2,256,1024]{2,3,1,0:T(8,128)(2,1)}, u32[]{:S(2)}) copy-start(bf16[2,2,256,1024]{2,3,1,0:T(8,128)(2,1)} %copy-done.8) | copy-start | bytes 6291460
  178.0 4.0 %copy-start.26 = (bf16[256,4,64]{2,0,1:T(8,128)(2,1)S(1)}, bf16[256,4,64]{2,0,1:T(8,128)(2,1)}, u32[]{:S(2)}) copy-start(bf16[256,4,64]{2,0,1:T(8,128)(2,1)} %copy.58) | copy-start | bytes 393220
  178.0 4.0 %copy-start.27 = (bf16[256,4,64]{2,0,1:T(8,128)(2,1)S(1)}, bf16[256,4,64]{2,0,1:T(8,128)(2,1)}, u32[]{:S(2)}) copy-start(bf16[256,4,64]{2,0,1:T(8,128)(2,1)} %copy.57) | copy-start | bytes 393220
  180.3 7.2 %copy-start.2 = (bf16[256,4,128]{2,1,0:T(4,128)(2,1)}, bf16[256,4,128]{2,1,0:T(4,128)(2,1)S(1)}, u32[]{:S(2)}) copy-start(bf16[256,4,128]{2,1,0:T(4,128)(2,1)S(1)} %fusion.22) | copy-start | bytes 786436
  181.9 1.2 copy-start.14
  182.0 21.5 %collective-permute-start.12 = (bf16[1344,512]{1,0:T(8,128)(2,1)}, bf16[1344,512]{1,0:T(8,128)(2,1)}, u32[]{:S(2)}, u32[]{:S(2)}) collective-permute-start(bf16[1344,512]{1,0:T(8,128)(2,1)} %convolution_convert_fusion.5), channel_id=1, source_target_pairs={{0,4},{4,0},{8,12},{12,8},{1,5},{5,1},{9,13},{13,9},{2,6},{6,2},{1... | collective-permute-start | bytes 4128776 | tf_op jit(solution)/shard_map/ppermute | solution.py:26
  183.4 7.1 %collective-permute-start.11 = (bf16[256,512]{0,1:T(8,128)(2,1)S(1)}, bf16[256,512]{0,1:T(8,128)(2,1)S(1)}, u32[]{:S(2)}, u32[]{:S(2)}) collective-permute-start(bf16[256,512]{0,1:T(8,128)(2,1)S(1)} %get-tuple-element.33), channel_id=1, source_target_pairs={{4,0},{8,4},{12,8},{5,1},{9,5},{13,9},{6,2},{10,6},{14,10},{7,3},{... | collective-permute-start | bytes 786440 | tf_op jit(solution)/shard_map/ppermute | solution.py:21
  184.7 13.4 %collective-permute-start.10 = (bf16[256,512]{0,1:T(8,128)(2,1)S(1)}, bf16[256,512]{0,1:T(8,128)(2,1)S(1)}, u32[]{:S(2)}, u32[]{:S(2)}) collective-permute-start(bf16[256,512]{0,1:T(8,128)(2,1)S(1)} %get-tuple-element.34), channel_id=1, source_target_pairs={{8,0},{12,4},{9,1},{13,5},{10,2},{14,6},{11,3},{15,7},{24,16},{28,... | collective-permute-start | bytes 786440 | tf_op jit(solution)/shard_map/ppermute | solution.py:21
  186.0 13.9 %collective-permute-start.9 = (bf16[256,512]{0,1:T(8,128)(2,1)S(1)}, bf16[256,512]{0,1:T(8,128)(2,1)S(1)}, u32[]{:S(2)}, u32[]{:S(2)}) collective-permute-start(bf16[256,512]{0,1:T(8,128)(2,1)S(1)} %get-tuple-element.32), channel_id=1, source_target_pairs={{12,0},{13,1},{14,2},{15,3},{28,16},{29,17},{30,18},{31,19}} | collective-permute-start | bytes 786440 | tf_op jit(solution)/shard_map/ppermute | solution.py:21
  200.8 2.6 copy-start.3
  203.4 3.0 slice-start
  203.4 3.8 %copy-start.21 = (f32[256,512]{0,1:T(8,128)S(1)}, f32[256,512]{0,1:T(8,128)}, u32[]{:S(2)}) copy-start(f32[256,512]{0,1:T(8,128)} %fusion.26) | copy-start | bytes 1572868
  203.4 19.6 %collective-permute-start.13 = (bf16[512,1344]{0,1:T(8,128)(2,1)}, bf16[512,1344]{0,1:T(8,128)(2,1)}, u32[]{:S(2)}, u32[]{:S(2)}) collective-permute-start(bf16[512,1344]{0,1:T(8,128)(2,1)} %convolution_convert_fusion.4), channel_id=1, source_target_pairs={{0,4},{4,0},{8,12},{12,8},{1,5},{5,1},{9,13},{13,9},{2,6},{6,2},{1... | collective-permute-start | bytes 4128776 | tf_op jit(solution)/shard_map/ppermute | solution.py:26
  206.4 32.8 %collective-permute-start.14 = (bf16[1344,512]{1,0:T(8,128)(2,1)}, bf16[1344,512]{1,0:T(8,128)(2,1)}, u32[]{:S(2)}, u32[]{:S(2)}) collective-permute-start(bf16[1344,512]{1,0:T(8,128)(2,1)} %add_convert_fusion.1), channel_id=1, source_target_pairs={{0,8},{4,12},{8,0},{12,4},{1,9},{5,13},{9,1},{13,5},{2,10},{6,14},... | collective-permute-start | bytes 4128776 | tf_op jit(solution)/shard_map/ppermute | solution.py:26
  212.7 0.8 copy-start.18
  223.0 30.4 %copy-start.6 = (bf16[256,512]{0,1:T(8,128)(2,1)}, bf16[256,512]{0,1:T(8,128)(2,1)S(1)}, u32[]{:S(2)}) copy-start(bf16[256,512]{0,1:T(8,128)(2,1)S(1)} %pad_maximum_fusion.3) | copy-start | bytes 786436
  226.1 15.2 %copy-start.11 = (f32[256,1344]{0,1:T(8,128)S(1)}, f32[256,1344]{0,1:T(8,128)}, u32[]{:S(2)}) copy-start(f32[256,1344]{0,1:T(8,128)} %fusion.60) | copy-start | bytes 4128772
  239.3 32.1 %collective-permute-start.16 = (bf16[512,1344]{0,1:T(8,128)(2,1)}, bf16[512,1344]{0,1:T(8,128)(2,1)}, u32[]{:S(2)}, u32[]{:S(2)}) collective-permute-start(bf16[512,1344]{0,1:T(8,128)(2,1)} %add_convert_fusion), channel_id=1, source_target_pairs={{0,8},{4,12},{8,0},{12,4},{1,9},{5,13},{9,1},{13,5},{2,10},{6,14},... | collective-permute-start | bytes 4128776 | tf_op jit(solution)/shard_map/ppermute | solution.py:26
  245.9 1.9 copy-start.4
  258.1 1.6 copy-start.5
  259.6 11.7 %copy-start.7 = (bf16[256,512]{0,1:T(8,128)(2,1)S(1)}, bf16[256,512]{0,1:T(8,128)(2,1)}, u32[]{:S(2)}) copy-start(bf16[256,512]{0,1:T(8,128)(2,1)} %copy-done.6) | copy-start | bytes 786436
  259.6 12.3 %copy-start.28 = (bf16[256,2048]{0,1:T(8,128)(2,1)S(1)}, bf16[256,2048]{0,1:T(8,128)(2,1)}, u32[]{:S(2)}) copy-start(bf16[256,2048]{0,1:T(8,128)(2,1)} %all-gather.8.cloned.1.call-done) | copy-start | bytes 3145732
  259.6 20.9 %collective-permute-start.15 = (bf16[1344,512]{1,0:T(8,128)(2,1)S(1)}, bf16[1344,512]{1,0:T(8,128)(2,1)S(1)}, u32[]{:S(2)}, u32[]{:S(2)}) collective-permute-start(bf16[1344,512]{1,0:T(8,128)(2,1)S(1)} %convolution_convert_fusion.3), channel_id=1, source_target_pairs={{0,4},{4,0},{8,12},{12,8},{1,5},{5,1},{9,13},{13,9},{2,6},{6,2},{1... | collective-permute-start | bytes 4128776 | tf_op jit(solution)/shard_map/ppermute | solution.py:26
  271.9 7.5 %collective-permute-start.18 = (bf16[1344,512]{1,0:T(8,128)(2,1)S(1)}, bf16[1344,512]{1,0:T(8,128)(2,1)S(1)}, u32[]{:S(2)}, u32[]{:S(2)}) collective-permute-start(bf16[1344,512]{1,0:T(8,128)(2,1)S(1)} %convolution_convert_fusion.1), channel_id=1, source_target_pairs={{0,4},{4,0},{8,12},{12,8},{1,5},{5,1},{9,13},{13,9},{2,6},{6,2},{1... | collective-permute-start | bytes 4128776 | tf_op jit(solution)/shard_map/ppermute | solution.py:26
  272.5 11.4 %collective-permute-start.20 = (bf16[512,1344]{0,1:T(8,128)(2,1)S(1)}, bf16[512,1344]{0,1:T(8,128)(2,1)S(1)}, u32[]{:S(2)}, u32[]{:S(2)}) collective-permute-start(bf16[512,1344]{0,1:T(8,128)(2,1)S(1)} %convolution_convert_fusion), channel_id=1, source_target_pairs={{0,4},{4,0},{8,12},{12,8},{1,5},{5,1},{9,13},{13,9},{2,6},{6,2},{1... | collective-permute-start | bytes 4128776 | tf_op jit(solution)/shard_map/ppermute | solution.py:26
  279.3 8.1 %collective-permute-start.17 = (bf16[1344,512]{1,0:T(8,128)(2,1)S(1)}, bf16[1344,512]{1,0:T(8,128)(2,1)S(1)}, u32[]{:S(2)}, u32[]{:S(2)}) collective-permute-start(bf16[1344,512]{1,0:T(8,128)(2,1)S(1)} %convolution_convert_fusion.2), channel_id=1, source_target_pairs={{0,4},{4,0},{8,12},{12,8},{1,5},{5,1},{9,13},{13,9},{2,6},{6,2},{1... | collective-permute-start | bytes 4128776 | tf_op jit(solution)/shard_map/ppermute | solution.py:26
  279.9 32.6 %collective-permute-start.19 = (bf16[1344,512]{1,0:T(8,128)(2,1)S(1)}, bf16[1344,512]{1,0:T(8,128)(2,1)S(1)}, u32[]{:S(2)}, u32[]{:S(2)}) collective-permute-start(bf16[1344,512]{1,0:T(8,128)(2,1)S(1)} %fusion.6), channel_id=1, source_target_pairs={{0,8},{4,12},{8,0},{12,4},{1,9},{5,13},{9,1},{13,5},{2,10},{6,14},... | collective-permute-start | bytes 4128776 | tf_op jit(solution)/shard_map/ppermute | solution.py:26
  (1 other events, 0.7 us)
Sparse Core Ops, SparseCore 0:
  9.6 59.6 all-gather.3
  70.9 44.5 all-gather.5
  122.6 29.4 reduce-scatter.2
  162.2 26.5 all-gather.7
  258.2 53.0 reduce-scatter.4

commit v2 on v1

--- a/solution.py
+++ b/solution.py
@@ -240,18 +240,17 @@
     kv_back, (out_sums,) = ordered(kv_back, out_sums)
     query_near, query_far = exchange_far(query_sums, "tok")
     out_near, out_far = exchange_far(out_sums, "tok")
-    kv_later, query_far = lax.optimization_barrier((kv_back, query_far))
     kv_last, out_far = lax.optimization_barrier((kv_back, out_far))
     block_rows = jnp.zeros((TOK_DEV, full_rows.shape[1]), jnp.bfloat16)
     for offset in range(len(query_pieces)):
-        kv_used = kv_back if 2 * offset < len(query_pieces) else kv_later
         product = jnp.einsum(
             "tc,dc->td", query_back, query_pieces[offset], preferred_element_type=jnp.float32
-        ) + jnp.einsum("tc,dc->td", kv_used, kv_pieces[offset], preferred_element_type=jnp.float32)
+        ) + jnp.einsum("tc,dc->td", kv_back, kv_pieces[offset], preferred_element_type=jnp.float32)
         start = (block_index ^ offset) * height
         block_rows = lax.dynamic_update_slice_in_dim(
             block_rows, product.astype(jnp.bfloat16), start, 1
         )
+    block_rows, query_far = lax.optimization_barrier((block_rows, query_far))
     grad_x = lax.psum_scatter(block_rows, "hid", scatter_dimension=1, tiled=True)
     kv_sums = begin_scatter(full_rows, kv_last, "tok")
     grad_wq = finish((query_near, query_far))

time: 323 us -> 336 us (1.040)
  waiting for transfers between devices: 126 us -> 137 us
    ppermute x15, waiting for transfers between devices: 106 us -> 117 us  [swapped(): lax.ppermute(value, axis, [(source, source ^ bit) for source in range(cou...]
  transfers between devices with their start and end apart: 26 -> 26, of which waited for: 8 -> 8; matrix products, arithmetic and copies ran while one was open for 46% -> 44% of each run, Pallas kernels for 0% -> 0%
where the time goes in v2:
time: 336 us; the launch traced here: 334 us
  waiting for transfers between devices  137 us (41%)
  matrix products  77.3 us (23%)
  local copies, waits for them, and re-layouts  45.2 us (13%)
  other arithmetic  40.4 us (12%)
  starting transfers between devices  19.8 us (6%)
  between operations  14.5 us (4%)
    ppermute x15, waiting for transfers between devices, swapped(): lax.ppermute(value, axis, [(source, source ^ bit) for source in range(cou...  117 us
    dot_general x8, matrix products, project(): total = total + jnp.dot(columns, piece, preferred_element_type=jnp.float32)  17.5 us
    dot_general x12, matrix products, product(): jnp.einsum('td,tc->dc', picked, right, preferred_element_type=jnp.float32)  15.8 us
    unnamed x82, local copies, waits for them, and re-layouts  13.7 us
    ppermute x6, starting transfers between devices, shifted(): lax.ppermute(value, axis, [(source, source + steps) for source in range(f...  12.7 us
    dot_general x4, matrix products, local(): jnp.einsum('tc,dc->td', query_back, query_pieces[offset], preferred_eleme...  11.3 us
    ppermute x6, waiting for transfers between devices, shifted(): lax.ppermute(value, axis, [(source, source + steps) for source in range(f...  9.37 us
    reduce_scatter x1, waiting for transfers between devices, local(): lax.psum_scatter(partial_heads, 'hid', scatter_dimension=1, tiled=True)  9.2 us
  transfers between devices with their start and end apart: 26, of which 8 were waited for; matrix products, arithmetic and copies ran while one was open for 44% of the time, Pallas kernels for 0%

profile of v2, /device:TPU:0, one launch (start us, length us, event | category | flops | bytes accessed | tf_op | source)
XLA Modules:
  0.0 334.3 jit_solution(11016410429044273175)
XLA Ops:
  10.5 3.0 collective-permute-start.1
  14.2 30.6 %collective-permute-done.1 = bf16[1344,512]{1,0:T(8,128)(2,1)} collective-permute-done((bf16[1344,512]{1,0:T(8,128)(2,1)}, bf16[1344,512]{1,0:T(8,128)(2,1)}, u32[]{:S(2)}, u32[]{:S(2)}) %collective-permute-start.1) | collective-permute-done | bytes 1376288 | tf_op jit(solution)/shard_map/ppermute | solution.py:26
  46.1 1.5 fusion.19
  47.6 25.8 %collective-permute-done.7 = bf16[1344,512]{1,0:T(8,128)(2,1)} collective-permute-done((bf16[1344,512]{1,0:T(8,128)(2,1)}, bf16[1344,512]{1,0:T(8,128)(2,1)}, u32[]{:S(2)}, u32[]{:S(2)}) %collective-permute-start.7) | collective-permute-done | bytes 1376288 | tf_op jit(solution)/shard_map/ppermute | solution.py:26
  73.5 2.1 fusion.50
  75.7 2.5 convolution_add_fusion.11
  78.6 2.3 convolution_add_fusion.10
  81.0 1.9 convolution_add_fusion.9
  84.4 1.8 reshape.229
  86.2 2.0 multiply_reduce_fusion.3
  94.9 3.0 collective-permute-start.5
  97.9 3.6 %collective-permute-start.4 = (bf16[256,512]{1,0:T(8,128)(2,1)}, bf16[256,512]{1,0:T(8,128)(2,1)}, u32[]{:S(2)}, u32[]{:S(2)}) collective-permute-start(bf16[256,512]{1,0:T(8,128)(2,1)} %pad_maximum_fusion.1), channel_id=1, source_target_pairs={{0,8},{4,12},{1,9},{5,13},{2,10},{6,14},{3,11},{7,15},{16,24},{20,... | collective-permute-start | bytes 786440 | tf_op jit(solution)/shard_map/ppermute | solution.py:21
  101.5 2.0 collective-permute-start.3
  103.5 1.9 fusion.48
  105.4 1.9 convolution_add_fusion.8
  107.4 1.9 convolution_add_fusion.7
  109.3 2.7 convolution_add_fusion.6
  112.1 2.0 reshape.232
  114.1 2.0 multiply_reduce_fusion.1
  117.1 5.3 %convolution_convert_fusion.7 = bf16[256,2048]{1,0:T(8,128)(2,1)} fusion(bf16[256,1344]{0,1:T(8,128)(2,1)S(1)} %copy-done, bf16[2048,1344]{0,1:T(8,128)(2,1)} %all-gather.6.cloned.1.call-done), kind=kOutput, calls=%fused_computation.35 | convolution fusion | flops 1409810432 | bytes 7241728 | tf_op jit(solution)/shard_map/td,hd->th/dot_general | solution.py:143
  130.2 2.0 reshape.230
  132.2 2.0 reshape.231
  134.2 2.0 copy.82
  136.2 2.7 fusion.4
  138.9 2.0 copy-done.15
  141.0 1.9 convolution_convert_fusion.8
  142.9 9.2 %reduce-scatter.3.cloned.1.call-done = bf16[256,512]{1,0:T(8,128)(2,1)} async-done(((bf16[256,2048]{1,0:T(8,128)(2,1)}), bf16[256,512]{1,0:T(8,128)(2,1)}) %reduce-scatter.3.cloned.1.call-update) | async-done | bytes 262160 | tf_op jit(solution)/shard_map/reduce_scatter | solution.py:145
  152.1 1.8 copy.103
  153.9 5.9 %fusion = (f32[2,2,256]{2,1,0:T(2,128)S(1)}, f32[2,1024,256,2]{2,1,3,0:T(8,128)}) fusion(f32[2,2,256]{2,1,0:T(2,128)S(1)} %get-tuple-element.49, f32[2,1024,256,2]{2,1,3,0:T(8,128)} %copy-done.15, pred[256,1024]{0,1:T(8,128)(4,1)} %fusion.19, bf16[256,2,2,128]{0,3,2,1:T(8,128)(2,1)} %bitcast.138, bf16[1024,2,128,1]{2,1,0,3:T(2,128)(2,1)} %bitcast.134), kind=kOutput, calls=%fused_computation.2 | convolution fusion | flops 273677312 | bytes 9445376 | tf_op jit(solution)/shard_map/tkgd,ukd->kgtu/dot_general | solution.py:191
  159.7 2.3 fusion.16
  162.1 4.7 %fusion.2 = bf16[2,2,256,1024]{2,3,1,0:T(8,128)(2,1)S(1)} fusion(f32[2,1024,256,2]{2,1,3,0:T(8,128)} %get-tuple-element.52, f32[2,2,256]{2,1,0:T(2,128)S(1)} %get-tuple-element.51, f32[2,2,256]{2,1,0:T(2,128)S(1)} %get-tuple-element.49, f32[2,1024,256,2]{2,1,3,0:T(8,128)} %copy-done.15, pred[256,1024]{0,1:T(8,128)(4,1)} %fusion.19), kind=kLoop, calls=%fused_computation.4 | loop fusion | flops 7340032 | bytes 10756096 | tf_op jit(solution)/shard_map/convert_element_type | solution.py:199
  168.3 2.0 copy.100
  170.3 1.9 copy.99
  172.3 1.6 multiply_add_fusion.1
  178.0 2.3 fusion.22
  180.3 1.6 convolution_convert_fusion.5
  187.5 3.0 fusion.60
  190.5 7.6 %collective-permute-done.10 = bf16[256,512]{0,1:T(8,128)(2,1)S(1)} collective-permute-done((bf16[256,512]{0,1:T(8,128)(2,1)S(1)}, bf16[256,512]{0,1:T(8,128)(2,1)S(1)}, u32[]{:S(2)}, u32[]{:S(2)}) %collective-permute-start.10) | collective-permute-done | bytes 262176 | tf_op jit(solution)/shard_map/ppermute | solution.py:21
  198.1 1.7 collective-permute-done.9
  200.8 2.6 convolution_convert_fusion.4
  203.4 3.0 add_convert_fusion.1
  207.8 1.7 copy.102
  209.6 1.7 copy.101
  213.5 2.2 multiply_reduce_fusion.2
  217.6 2.7 fusion.52
  220.3 1.7 copy.98
  223.0 3.1 add_convert_fusion
  226.1 2.0 collective-permute-start.16
  228.2 1.7 broadcast_in_dim.16
  229.9 2.7 fusion.14
  232.6 1.8 fusion.113
  234.5 1.9 fusion.114
  236.4 2.7 fusion.8
  239.1 2.8 fusion.10
  242.0 1.9 fusion.115
  243.8 2.8 fusion.12
  246.6 8.6 %collective-permute-done.14 = bf16[1344,512]{1,0:T(8,128)(2,1)} collective-permute-done((bf16[1344,512]{1,0:T(8,128)(2,1)}, bf16[1344,512]{1,0:T(8,128)(2,1)}, u32[]{:S(2)}, u32[]{:S(2)}) %collective-permute-start.14) | collective-permute-done | bytes 1376288 | tf_op jit(solution)/shard_map/ppermute | solution.py:26
  255.3 1.5 convolution_convert_fusion.3
  257.5 26.8 %collective-permute-done.16 = bf16[512,1344]{0,1:T(8,128)(2,1)} collective-permute-done((bf16[512,1344]{0,1:T(8,128)(2,1)}, bf16[512,1344]{0,1:T(8,128)(2,1)}, u32[]{:S(2)}, u32[]{:S(2)}) %collective-permute-start.16) | collective-permute-done | bytes 1376288 | tf_op jit(solution)/shard_map/ppermute | solution.py:26
  286.1 5.0 %convolution_convert_fusion.6 = bf16[256,1344]{0,1:T(8,128)(2,1)} fusion(bf16[2048,1344]{0,1:T(8,128)(2,1)} %all-gather.6.cloned.1.call-done, bf16[256,2048]{0,1:T(8,128)(2,1)S(1)} %copy-done.28), kind=kOutput, calls=%fused_computation.34 | convolution fusion | flops 1409630208 | bytes 7241728 | tf_op jit(solution)/shard_map/dot_general | solution.py:188
  293.3 3.4 %convert_add_fusion.1 = f32[1344,512]{1,0:T(8,128)} fusion(bf16[1344,512]{1,0:T(8,128)(2,1)} %collective-permute-done.14, f32[1344,512]{1,0:T(8,128)S(1)} %fusion.46, bf16[1344,512]{1,0:T(8,128)(2,1)S(1)} %collective-permute-done.15), kind=kLoop, calls=%fused_computation.23 | loop fusion | flops 2752512 | bytes 8257536 | tf_op jit(solution)/shard_map/add | solution.py:75
  296.7 3.4 %convert_add_fusion = f32[512,1344]{0,1:T(8,128)} fusion(bf16[512,1344]{0,1:T(8,128)(2,1)} %collective-permute-done.16, f32[512,1344]{0,1:T(8,128)S(1)} %fusion.63, bf16[512,1344]{0,1:T(8,128)(2,1)S(1)} %collective-permute-done.20), kind=kLoop, calls=%fused_computation.22 | loop fusion | flops 2752512 | bytes 8257536 | tf_op jit(solution)/shard_map/add | solution.py:75
  300.2 25.3 %collective-permute-done.19 = bf16[1344,512]{1,0:T(8,128)(2,1)S(1)} collective-permute-done((bf16[1344,512]{1,0:T(8,128)(2,1)S(1)}, bf16[1344,512]{1,0:T(8,128)(2,1)S(1)}, u32[]{:S(2)}, u32[]{:S(2)}) %collective-permute-start.19) | collective-permute-done | bytes 1376288 | tf_op jit(solution)/shard_map/ppermute | solution.py:26
  326.1 1.7 fusion.107
  (171 shorter events, 46.1 us)
Async XLA Ops:
  7.2 109.9 %copy-start = (bf16[256,1344]{0,1:T(8,128)(2,1)S(1)}, bf16[256,1344]{0,1:T(8,128)(2,1)}, u32[]{:S(2)}) copy-start(bf16[256,1344]{0,1:T(8,128)(2,1)} %param.17) | copy-start | bytes 2064388
  7.2 1.6 copy-start.31
  7.2 2.5 copy-start.32
  7.2 66.3 %all-gather.4.cloned.1.call-start = ((), (), s32[]{:S(2)}) async-start(), calls=%async_computation.2 | async-start | bytes 3440640 | tf_op jit(solution)/shard_map/all_gather | solution.py:125
  7.9 6.1 %copy-start.35 = (s32[1024]{0:T(1024)S(1)}, s32[1024]{0:T(1024)}, u32[]{:S(2)}) copy-start(s32[1024]{0:T(1024)} %param.16) | copy-start | bytes 12292
  7.9 109.2 %all-gather.6.cloned.1.call-start = ((), (), s32[]{:S(2)}) async-start(), calls=%async_computation.3 | async-start | bytes 6881280 | tf_op jit(solution)/shard_map/all_gather | solution.py:128
  8.7 143.4 %reduce-scatter.3.cloned.1.call-start = ((), (), s32[]{:S(2)}) async-start(), calls=%async_computation.4 | async-start | bytes 1310720 | tf_op jit(solution)/shard_map/reduce_scatter | solution.py:145
  10.5 34.3 %collective-permute-start.1 = (bf16[1344,512]{1,0:T(8,128)(2,1)}, bf16[1344,512]{1,0:T(8,128)(2,1)}, u32[]{:S(2)}, u32[]{:S(2)}) collective-permute-start(bf16[1344,512]{1,0:T(8,128)(2,1)} %constant_dynamic-update-slice_fusion), channel_id=1, source_target_pairs={{0,8},{4,12},{8,0},{12,4},{1,9},{5,13},{9,1},{13,5},{2,10},{6,14},... | collective-permute-start | bytes 4128776 | tf_op jit(solution)/shard_map/ppermute | solution.py:26
  13.5 60.0 %collective-permute-start.7 = (bf16[1344,512]{1,0:T(8,128)(2,1)}, bf16[1344,512]{1,0:T(8,128)(2,1)}, u32[]{:S(2)}, u32[]{:S(2)}) collective-permute-start(bf16[1344,512]{1,0:T(8,128)(2,1)} %param.10), channel_id=1, source_target_pairs={{0,8},{4,12},{8,0},{12,4},{1,9},{5,13},{9,1},{13,5},{2,10},{6,14},... | collective-permute-start | bytes 4128776 | tf_op jit(solution)/shard_map/ppermute | solution.py:26
  13.5 62.1 %collective-permute-start = (bf16[1344,512]{1,0:T(8,128)(2,1)}, bf16[1344,512]{1,0:T(8,128)(2,1)}, u32[]{:S(2)}, u32[]{:S(2)}) collective-permute-start(bf16[1344,512]{1,0:T(8,128)(2,1)} %constant_dynamic-update-slice_fusion), channel_id=1, source_target_pairs={{0,4},{4,0},{8,12},{12,8},{1,5},{5,1},{9,13},{13,9},{2,6},{6,2},{1... | collective-permute-start | bytes 4128776 | tf_op jit(solution)/shard_map/ppermute | solution.py:26
  13.5 91.9 %collective-permute-start.6 = (bf16[1344,512]{1,0:T(8,128)(2,1)}, bf16[1344,512]{1,0:T(8,128)(2,1)}, u32[]{:S(2)}, u32[]{:S(2)}) collective-permute-start(bf16[1344,512]{1,0:T(8,128)(2,1)} %param.10), channel_id=1, source_target_pairs={{0,4},{4,0},{8,12},{12,8},{1,5},{5,1},{9,13},{13,9},{2,6},{6,2},{1... | collective-permute-start | bytes 4128776 | tf_op jit(solution)/shard_map/ppermute | solution.py:26
  44.8 36.1 %collective-permute-start.2 = (bf16[1344,512]{1,0:T(8,128)(2,1)}, bf16[1344,512]{1,0:T(8,128)(2,1)}, u32[]{:S(2)}, u32[]{:S(2)}) collective-permute-start(bf16[1344,512]{1,0:T(8,128)(2,1)} %collective-permute-done.1), channel_id=1, source_target_pairs={{0,4},{4,0},{8,12},{12,8},{1,5},{5,1},{9,13},{13,9},{2,6},{6,2},{1... | collective-permute-start | bytes 4128776 | tf_op jit(solution)/shard_map/ppermute | solution.py:26
  73.5 35.8 %collective-permute-start.8 = (bf16[1344,512]{1,0:T(8,128)(2,1)}, bf16[1344,512]{1,0:T(8,128)(2,1)}, u32[]{:S(2)}, u32[]{:S(2)}) collective-permute-start(bf16[1344,512]{1,0:T(8,128)(2,1)} %collective-permute-done.7), channel_id=1, source_target_pairs={{0,4},{4,0},{8,12},{12,8},{1,5},{5,1},{9,13},{13,9},{2,6},{6,2},{1... | collective-permute-start | bytes 4128776 | tf_op jit(solution)/shard_map/ppermute | solution.py:26
  75.6 3.0 copy-start.1
  81.0 9.0 %copy-start.37 = (f32[128]{0:T(128)S(1)}, f32[128]{0:T(128)}, u32[]{:S(2)}) copy-start(f32[128]{0:T(128)} %param.15) | copy-start | bytes 1540
  82.9 0.8 copy-start.20
  92.3 13.2 %copy-start.22 = (bf16[256,256]{1,0:T(8,128)(2,1)}, bf16[256,256]{1,0:T(8,128)(2,1)S(1)}, u32[]{:S(2)}) copy-start(bf16[256,256]{1,0:T(8,128)(2,1)S(1)} %slice.108) | copy-start | bytes 393220
  94.2 7.3 %copy-start.24 = (bf16[32,8,2,128]{3,1,2,0:T(8,128)(2,1)}, bf16[32,8,2,128]{3,1,2,0:T(8,128)(2,1)S(1)}, u32[]{:S(2)}) copy-start(bf16[32,8,2,128]{3,1,2,0:T(8,128)(2,1)S(1)} %copy.145) | copy-start | bytes 393220
  94.9 33.0 %collective-permute-start.5 = (bf16[256,512]{1,0:T(8,128)(2,1)}, bf16[256,512]{1,0:T(8,128)(2,1)}, u32[]{:S(2)}, u32[]{:S(2)}) collective-permute-start(bf16[256,512]{1,0:T(8,128)(2,1)} %pad_maximum_fusion.1), channel_id=1, source_target_pairs={{0,4},{4,8},{8,12},{1,5},{5,9},{9,13},{2,6},{6,10},{10,14},{3,7},{... | collective-permute-start | bytes 786440 | tf_op jit(solution)/shard_map/ppermute | solution.py:21
  97.9 30.1 %collective-permute-start.4 = (bf16[256,512]{1,0:T(8,128)(2,1)}, bf16[256,512]{1,0:T(8,128)(2,1)}, u32[]{:S(2)}, u32[]{:S(2)}) collective-permute-start(bf16[256,512]{1,0:T(8,128)(2,1)} %pad_maximum_fusion.1), channel_id=1, source_target_pairs={{0,8},{4,12},{1,9},{5,13},{2,10},{6,14},{3,11},{7,15},{16,24},{20,... | collective-permute-start | bytes 786440 | tf_op jit(solution)/shard_map/ppermute | solution.py:21
  101.5 26.5 %collective-permute-start.3 = (bf16[256,512]{1,0:T(8,128)(2,1)}, bf16[256,512]{1,0:T(8,128)(2,1)}, u32[]{:S(2)}, u32[]{:S(2)}) collective-permute-start(bf16[256,512]{1,0:T(8,128)(2,1)} %pad_maximum_fusion.1), channel_id=1, source_target_pairs={{0,12},{1,13},{2,14},{3,15},{16,28},{17,29},{18,30},{19,31}} | collective-permute-start | bytes 786440 | tf_op jit(solution)/shard_map/ppermute | solution.py:21
  117.1 6.4 %copy-start.36 = (f32[128]{0:T(128)S(1)}, f32[128]{0:T(128)}, u32[]{:S(2)}) copy-start(f32[128]{0:T(128)} %param.14) | copy-start | bytes 1540
  122.5 78.3 %all-gather.8.cloned.1.call-start = ((), (), s32[]{:S(2)}) async-start(), calls=%async_computation.5 | async-start | bytes 1310720 | tf_op jit(solution)/shard_map/all_gather | solution.py:187
  123.6 4.4 %copy-start.23 = (bf16[256,256]{1,0:T(8,128)(2,1)S(1)}, bf16[256,256]{1,0:T(8,128)(2,1)}, u32[]{:S(2)}) copy-start(bf16[256,256]{1,0:T(8,128)(2,1)} %copy-done.22) | copy-start | bytes 393220
  123.6 4.4 %copy-start.25 = (bf16[32,8,2,128]{3,1,2,0:T(8,128)(2,1)S(1)}, bf16[32,8,2,128]{3,1,2,0:T(8,128)(2,1)}, u32[]{:S(2)}) copy-start(bf16[32,8,2,128]{3,1,2,0:T(8,128)(2,1)} %copy-done.24) | copy-start | bytes 393220
  136.2 4.7 %copy-start.29 = (pred[256,1024]{0,1:T(8,128)(4,1)S(1)}, pred[256,1024]{0,1:T(8,128)(4,1)}, u32[]{:S(2)}) copy-start(pred[256,1024]{0,1:T(8,128)(4,1)} %fusion.19) | copy-start | bytes 786436
  136.2 4.7 %copy-start.33 = (bf16[1024,2,128]{2,1,0:T(2,128)(2,1)S(1)}, bf16[1024,2,128]{2,1,0:T(2,128)(2,1)}, u32[]{:S(2)}) copy-start(bf16[1024,2,128]{2,1,0:T(2,128)(2,1)} %reshape.230) | copy-start | bytes 1572868
  138.9 2.1 copy-start.15
  153.9 5.9 %copy-start.16 = (f32[2,1024,256,2]{2,1,3,0:T(8,128)S(1)}, f32[2,1024,256,2]{2,1,3,0:T(8,128)}, u32[]{:S(2)}) copy-start(f32[2,1024,256,2]{2,1,3,0:T(8,128)} %copy-done.15) | copy-start | bytes 12582916
  153.9 5.9 %copy-start.30 = (pred[256,1024]{0,1:T(8,128)(4,1)S(1)}, pred[256,1024]{0,1:T(8,128)(4,1)}, u32[]{:S(2)}) copy-start(pred[256,1024]{0,1:T(8,128)(4,1)} %fusion.19) | copy-start | bytes 786436
  153.9 5.9 %copy-start.34 = (bf16[256,512]{0,1:T(8,128)(2,1)S(1)}, bf16[256,512]{0,1:T(8,128)(2,1)}, u32[]{:S(2)}) copy-start(bf16[256,512]{0,1:T(8,128)(2,1)} %copy.103) | copy-start | bytes 786436
  162.0 165.8 %reduce-scatter.5.cloned.1.call-start = ((), (), s32[]{:S(2)}) async-start(), calls=%async_computation.6 | async-start | bytes 3440640 | tf_op jit(solution)/shard_map/reduce_scatter | solution.py:254
  162.1 4.8 %copy-start.19 = (bf16[1024,2,128,1]{0,2,3,1:T(8,128)(2,1)S(1)}, bf16[1024,2,128,1]{0,2,3,1:T(8,128)(2,1)}, u32[]{:S(2)}) copy-start(bf16[1024,2,128,1]{0,2,3,1:T(8,128)(2,1)} %copy.82) | copy-start | bytes 1572868
  166.9 1.5 copy-start.8
  172.3 2.6 copy-start.10
  173.9 0.8 copy-start.12
  173.9 1.0 copy-start.13
  178.0 4.0 %copy-start.9 = (bf16[2,2,256,1024]{2,3,1,0:T(8,128)(2,1)S(1)}, bf16[2,2,256,1024]{2,3,1,0:T(8,128)(2,1)}, u32[]{:S(2)}) copy-start(bf16[2,2,256,1024]{2,3,1,0:T(8,128)(2,1)} %copy-done.8) | copy-start | bytes 6291460
  178.0 4.0 %copy-start.26 = (bf16[256,4,64]{2,0,1:T(8,128)(2,1)S(1)}, bf16[256,4,64]{2,0,1:T(8,128)(2,1)}, u32[]{:S(2)}) copy-start(bf16[256,4,64]{2,0,1:T(8,128)(2,1)} %copy.58) | copy-start | bytes 393220
  178.0 4.0 %copy-start.27 = (bf16[256,4,64]{2,0,1:T(8,128)(2,1)S(1)}, bf16[256,4,64]{2,0,1:T(8,128)(2,1)}, u32[]{:S(2)}) copy-start(bf16[256,4,64]{2,0,1:T(8,128)(2,1)} %copy.57) | copy-start | bytes 393220
  180.3 7.2 %copy-start.2 = (bf16[256,4,128]{2,1,0:T(4,128)(2,1)}, bf16[256,4,128]{2,1,0:T(4,128)(2,1)S(1)}, u32[]{:S(2)}) copy-start(bf16[256,4,128]{2,1,0:T(4,128)(2,1)S(1)} %fusion.22) | copy-start | bytes 786436
  181.9 1.2 copy-start.14
  182.0 21.5 %collective-permute-start.12 = (bf16[1344,512]{1,0:T(8,128)(2,1)}, bf16[1344,512]{1,0:T(8,128)(2,1)}, u32[]{:S(2)}, u32[]{:S(2)}) collective-permute-start(bf16[1344,512]{1,0:T(8,128)(2,1)} %convolution_convert_fusion.5), channel_id=1, source_target_pairs={{0,4},{4,0},{8,12},{12,8},{1,5},{5,1},{9,13},{13,9},{2,6},{6,2},{1... | collective-permute-start | bytes 4128776 | tf_op jit(solution)/shard_map/ppermute | solution.py:26
  183.4 7.1 %collective-permute-start.11 = (bf16[256,512]{0,1:T(8,128)(2,1)S(1)}, bf16[256,512]{0,1:T(8,128)(2,1)S(1)}, u32[]{:S(2)}, u32[]{:S(2)}) collective-permute-start(bf16[256,512]{0,1:T(8,128)(2,1)S(1)} %get-tuple-element.33), channel_id=1, source_target_pairs={{4,0},{8,4},{12,8},{5,1},{9,5},{13,9},{6,2},{10,6},{14,10},{7,3},{... | collective-permute-start | bytes 786440 | tf_op jit(solution)/shard_map/ppermute | solution.py:21
  184.7 13.4 %collective-permute-start.10 = (bf16[256,512]{0,1:T(8,128)(2,1)S(1)}, bf16[256,512]{0,1:T(8,128)(2,1)S(1)}, u32[]{:S(2)}, u32[]{:S(2)}) collective-permute-start(bf16[256,512]{0,1:T(8,128)(2,1)S(1)} %get-tuple-element.34), channel_id=1, source_target_pairs={{8,0},{12,4},{9,1},{13,5},{10,2},{14,6},{11,3},{15,7},{24,16},{28,... | collective-permute-start | bytes 786440 | tf_op jit(solution)/shard_map/ppermute | solution.py:21
  186.0 13.9 %collective-permute-start.9 = (bf16[256,512]{0,1:T(8,128)(2,1)S(1)}, bf16[256,512]{0,1:T(8,128)(2,1)S(1)}, u32[]{:S(2)}, u32[]{:S(2)}) collective-permute-start(bf16[256,512]{0,1:T(8,128)(2,1)S(1)} %get-tuple-element.32), channel_id=1, source_target_pairs={{12,0},{13,1},{14,2},{15,3},{28,16},{29,17},{30,18},{31,19}} | collective-permute-start | bytes 786440 | tf_op jit(solution)/shard_map/ppermute | solution.py:21
  200.8 2.6 copy-start.3
  203.4 3.0 copy-start.21
  203.4 3.7 %slice-start = ((f32[256,512]{0,1:T(8,128)}), f32[256,256]{0,1:T(8,128)S(1)}, s32[]{:S(2)}) async-start(f32[256,512]{0,1:T(8,128)} %fusion.26), calls=%async_computation.7 | async-start | bytes 524288 | tf_op jit(solution)/shard_map/slice | solution.py:233
  203.4 19.6 %collective-permute-start.13 = (bf16[512,1344]{0,1:T(8,128)(2,1)}, bf16[512,1344]{0,1:T(8,128)(2,1)}, u32[]{:S(2)}, u32[]{:S(2)}) collective-permute-start(bf16[512,1344]{0,1:T(8,128)(2,1)} %convolution_convert_fusion.4), channel_id=1, source_target_pairs={{0,4},{4,0},{8,12},{12,8},{1,5},{5,1},{9,13},{13,9},{2,6},{6,2},{1... | collective-permute-start | bytes 4128776 | tf_op jit(solution)/shard_map/ppermute | solution.py:26
  212.7 0.8 copy-start.18
  222.0 33.3 %collective-permute-start.14 = (bf16[1344,512]{1,0:T(8,128)(2,1)}, bf16[1344,512]{1,0:T(8,128)(2,1)}, u32[]{:S(2)}, u32[]{:S(2)}) collective-permute-start(bf16[1344,512]{1,0:T(8,128)(2,1)} %add_convert_fusion.1), channel_id=1, source_target_pairs={{0,8},{4,12},{8,0},{12,4},{1,9},{5,13},{9,1},{13,5},{2,10},{6,14},... | collective-permute-start | bytes 4128776 | tf_op jit(solution)/shard_map/ppermute | solution.py:26
  223.0 19.0 %copy-start.6 = (bf16[256,512]{0,1:T(8,128)(2,1)}, bf16[256,512]{0,1:T(8,128)(2,1)S(1)}, u32[]{:S(2)}) copy-start(bf16[256,512]{0,1:T(8,128)(2,1)S(1)} %pad_maximum_fusion.3) | copy-start | bytes 786436
  226.1 3.8 %copy-start.11 = (f32[256,1344]{0,1:T(8,128)S(1)}, f32[256,1344]{0,1:T(8,128)}, u32[]{:S(2)}) copy-start(f32[256,1344]{0,1:T(8,128)} %fusion.60) | copy-start | bytes 4128772
  226.1 58.2 %collective-permute-start.16 = (bf16[512,1344]{0,1:T(8,128)(2,1)}, bf16[512,1344]{0,1:T(8,128)(2,1)}, u32[]{:S(2)}, u32[]{:S(2)}) collective-permute-start(bf16[512,1344]{0,1:T(8,128)(2,1)} %add_convert_fusion), channel_id=1, source_target_pairs={{0,8},{4,12},{8,0},{12,4},{1,9},{5,13},{9,1},{13,5},{2,10},{6,14},... | collective-permute-start | bytes 4128776 | tf_op jit(solution)/shard_map/ppermute | solution.py:26
  234.5 1.9 copy-start.4
  255.3 1.7 copy-start.5
  256.9 27.4 %copy-start.7 = (bf16[256,512]{0,1:T(8,128)(2,1)S(1)}, bf16[256,512]{0,1:T(8,128)(2,1)}, u32[]{:S(2)}) copy-start(bf16[256,512]{0,1:T(8,128)(2,1)} %copy-done.6) | copy-start | bytes 786436
  256.9 28.1 %copy-start.28 = (bf16[256,2048]{0,1:T(8,128)(2,1)S(1)}, bf16[256,2048]{0,1:T(8,128)(2,1)}, u32[]{:S(2)}) copy-start(bf16[256,2048]{0,1:T(8,128)(2,1)} %all-gather.8.cloned.1.call-done) | copy-start | bytes 3145732
  256.9 36.4 %collective-permute-start.15 = (bf16[1344,512]{1,0:T(8,128)(2,1)S(1)}, bf16[1344,512]{1,0:T(8,128)(2,1)S(1)}, u32[]{:S(2)}, u32[]{:S(2)}) collective-permute-start(bf16[1344,512]{1,0:T(8,128)(2,1)S(1)} %convolution_convert_fusion.3), channel_id=1, source_target_pairs={{0,4},{4,0},{8,12},{12,8},{1,5},{5,1},{9,13},{13,9},{2,6},{6,2},{1... | collective-permute-start | bytes 4128776 | tf_op jit(solution)/shard_map/ppermute | solution.py:26
  284.9 7.4 %collective-permute-start.18 = (bf16[1344,512]{1,0:T(8,128)(2,1)S(1)}, bf16[1344,512]{1,0:T(8,128)(2,1)S(1)}, u32[]{:S(2)}, u32[]{:S(2)}) collective-permute-start(bf16[1344,512]{1,0:T(8,128)(2,1)S(1)} %convolution_convert_fusion.1), channel_id=1, source_target_pairs={{0,4},{4,0},{8,12},{12,8},{1,5},{5,1},{9,13},{13,9},{2,6},{6,2},{1... | collective-permute-start | bytes 4128776 | tf_op jit(solution)/shard_map/ppermute | solution.py:26
  285.5 11.2 %collective-permute-start.20 = (bf16[512,1344]{0,1:T(8,128)(2,1)S(1)}, bf16[512,1344]{0,1:T(8,128)(2,1)S(1)}, u32[]{:S(2)}, u32[]{:S(2)}) collective-permute-start(bf16[512,1344]{0,1:T(8,128)(2,1)S(1)} %convolution_convert_fusion), channel_id=1, source_target_pairs={{0,4},{4,0},{8,12},{12,8},{1,5},{5,1},{9,13},{13,9},{2,6},{6,2},{1... | collective-permute-start | bytes 4128776 | tf_op jit(solution)/shard_map/ppermute | solution.py:26
  292.2 8.0 %collective-permute-start.17 = (bf16[1344,512]{1,0:T(8,128)(2,1)S(1)}, bf16[1344,512]{1,0:T(8,128)(2,1)S(1)}, u32[]{:S(2)}, u32[]{:S(2)}) collective-permute-start(bf16[1344,512]{1,0:T(8,128)(2,1)S(1)} %convolution_convert_fusion.2), channel_id=1, source_target_pairs={{0,4},{4,0},{8,12},{12,8},{1,5},{5,1},{9,13},{13,9},{2,6},{6,2},{1... | collective-permute-start | bytes 4128776 | tf_op jit(solution)/shard_map/ppermute | solution.py:26
  292.9 32.6 %collective-permute-start.19 = (bf16[1344,512]{1,0:T(8,128)(2,1)S(1)}, bf16[1344,512]{1,0:T(8,128)(2,1)S(1)}, u32[]{:S(2)}, u32[]{:S(2)}) collective-permute-start(bf16[1344,512]{1,0:T(8,128)(2,1)S(1)} %fusion.6), channel_id=1, source_target_pairs={{0,8},{4,12},{8,0},{12,4},{1,9},{5,13},{9,1},{13,5},{2,10},{6,14},... | collective-permute-start | bytes 4128776 | tf_op jit(solution)/shard_map/ppermute | solution.py:26
  (1 other events, 0.7 us)
Sparse Core Ops, SparseCore 0:
  9.6 59.6 all-gather.3
  70.9 44.5 all-gather.5
  122.6 29.4 reduce-scatter.2
  162.2 26.5 all-gather.7
  255.4 51.8 reduce-scatter.4
